TPU v7x, 128 devices: a whole 4x4x4 slice. The times are simulated.
128 devices in a mesh: dom: 16 (over z, y), sub: 8 (over x, core).
Axes of the slice: x: 4, y: 4, z: 4, core: 2. Of those that a mesh axis runs over, the one named last changes fastest.
Arguments:
- a_vals: bfloat16 [4096, 4, 128, 128], P(('dom', 'sub')), may hold values from -0.5 to 8.5, as said below
- a_cols: int32 [4096, 4], P(('dom', 'sub')), may hold values from 0 to 47, as said below
- send_rows: int32 [128, 2, 8], P(('dom', 'sub')), may hold values from 0 to 31, as said below
- tentative: bfloat16 [4096, 128, 128], P(('dom', 'sub')), may hold values from -0.046875 to 0.046875
- p_cols: int32 [4096, 4], P(('dom', 'sub')), may hold values from 0 to 5, as said below
- ap_cols: int32 [4096, 4, 4], P(('dom', 'sub')), may hold values from 0 to 9, as said below
Outputs:
- coarse_matrix: float32 [4096, 1792], P(('dom', 'sub'))
Inputs may be any that keep to these rules, and one draw needn't show every extreme that they name: `send_rows`: the two lists of a partition name 16 distinct local tile rows. `a_cols`: entry 0 of a tile row's list is the row itself and a row's entries are distinct. Values below 32 are own rows; 32 + j is the j-th row of the upward list of the partition one slab lower with the same sub index, 40 + j the j-th row of the downward list of the partition one slab higher. Partitions of the first and last slab reference no missing neighbour. p_cols[i, m] = (slab of the row referenced by a_cols[i, m] - slab of i + 1) * 2 + the aggregate of that row within its slab; aggregates of a slab may gather rows of all its partitions. ap_cols[i, k, m] = p_cols[r, m] + (slab of r - slab of i + 1) * 2, where r is the row referenced by a_cols[i, k]. `a_vals`: the diagonal entries of each row's first tile are positive.
All inputs are finite; a program needn't handle non-finite values.
Results may differ from a plain program's by a relative error of at most 0.0007.
Values may be sent and summed in bfloat16 or wider, within the bound.
A program may use at most 128 MiB of HBM per device.

v0:
```python
import jax
import jax.numpy as jnp
from jax import lax
from jax.sharding import PartitionSpec as P

B = 128
K = 4
NCG = 2


OMEGA = 0.6


def extended(cells, sides, width):
    for axis, dim in sides:
        count = lax.axis_size(axis)
        ends = count - 1
        head = lax.slice_in_dim(cells, 0, width, axis=dim)
        tail = lax.slice_in_dim(cells, cells.shape[dim] - width, cells.shape[dim], axis=dim)
        cells = jnp.concatenate(
            [
                lax.ppermute(tail, axis, [(i, (i + 1) % count) for i in range(ends)]),
                cells,
                lax.ppermute(head, axis, [((i + 1) % count, i) for i in range(ends)]),
            ],
            axis=dim,
        )
    return cells


def block_terms(running, block_in, ext_smooth, col_ids, row_ids):
    blk_tiles, blk_cols, blk_smooth, blk_rows, blk_slots = block_in
    blk_count = blk_tiles.shape[0]
    fetched = ext_smooth[blk_cols]
    products = jnp.einsum(
        "tkxz,tkmzy->tkmxy", blk_tiles, fetched, preferred_element_type=jnp.float32
    )
    products = products.reshape(blk_count, K * K, B, B)
    pick_cols = (blk_slots.reshape(blk_count, K * K)[:, :, None] == col_ids).astype(jnp.float32)
    placed = jnp.einsum("tnc,tnxy->txcy", pick_cols, products, precision=lax.Precision.HIGHEST)
    placed = placed.reshape(blk_count, B, 5 * NCG * B).astype(jnp.bfloat16)
    weighted = jnp.einsum("tmzx,tzc->tmxc", blk_smooth, placed, preferred_element_type=jnp.float32)
    pick_slots = (blk_rows[:, :, None] == row_ids).astype(jnp.float32)
    update = jnp.einsum("tmr,tmxc->rxc", pick_slots, weighted, precision=lax.Precision.HIGHEST)
    return running + update


def assemble(rims):
    column_block = rims.shape[2] // 5
    return (
        jnp.pad(rims[0], ((0, 0), (0, 2 * column_block)))
        + jnp.pad(rims[2], ((0, 0), (column_block, column_block)))
        + jnp.pad(rims[4], ((0, 0), (2 * column_block, 0)))
    )


def on_device(a_vals, a_cols, send_rows, tentative, p_cols, ap_cols):
    ghosts = send_rows.shape[2]
    rows_here = a_vals.shape[0]
    list_rows = send_rows.reshape(2 * ghosts)
    outgoing = tentative[list_rows]
    arrived = extended(outgoing, (("dom", 0),), ghosts)
    ext_tentative = jnp.concatenate([tentative, arrived[:ghosts], arrived[3 * ghosts :]], 0)
    gathered = ext_tentative[a_cols]
    product = jnp.einsum("tkxz,tkzy->tkxy", a_vals, gathered, preferred_element_type=jnp.float32)
    inverse = 1.0 / jnp.diagonal(a_vals[:, 0], axis1=1, axis2=2).astype(jnp.float32)
    first_tile = (jnp.arange(K) == 0)[None, :, None, None]
    leading = jnp.where(
        first_tile, tentative[:, None].astype(jnp.float32), jnp.zeros((), jnp.float32)
    )
    smoothed = (leading - OMEGA * inverse[:, None, :, None] * product).astype(jnp.bfloat16)
    sent_rows = smoothed[list_rows]
    arrived_rows = extended(sent_rows, (("dom", 0),), ghosts)
    ext_smooth = jnp.concatenate([smoothed, arrived_rows[:ghosts], arrived_rows[3 * ghosts :]], 0)
    col_ids = jnp.arange(5 * NCG, dtype=jnp.int32)
    row_ids = jnp.arange(3 * NCG, dtype=jnp.int32)
    block_rows = 8
    blocks = rows_here // block_rows
    block_data = (
        a_vals.reshape(blocks, block_rows, K, B, B),
        a_cols.reshape(blocks, block_rows, K),
        smoothed.reshape(blocks, block_rows, K, B, B),
        p_cols.reshape(blocks, block_rows, K),
        ap_cols.reshape(blocks, block_rows, K, K),
    )

    def scan_step(running, block_in):
        return (block_terms(running, block_in, ext_smooth, col_ids, row_ids), None)

    start = jnp.zeros((3 * NCG, B, 5 * NCG * B), jnp.float32)
    running, unused = lax.scan(scan_step, start, block_data)
    partial_value = running.reshape(3, NCG * B, 5 * NCG * B)
    rims = extended(partial_value, (("dom", 0),), 1)
    coarse_band = assemble(rims)
    return lax.psum_scatter(coarse_band, "sub", scatter_dimension=0, tiled=True)


def solution(mesh):
    placed = (
        P(("dom", "sub"), None, None, None),
        P(("dom", "sub"), None),
        P(("dom", "sub"), None, None),
        P(("dom", "sub"), None, None),
        P(("dom", "sub"), None),
        P(("dom", "sub"), None, None),
    )
    return jax.shard_map(
        on_device, mesh=mesh, in_specs=placed, out_specs=P(("dom", "sub"), None), check_vma=False
    )
```

profile of v0, /device:TPU:0, one launch (start us, length us, event | category | flops | bytes accessed | tf_op | source)
XLA Modules:
  0.0 500.6 jit_solution(9938523201572014657)
XLA Ops:
  6.5 0.8 reshape.104
  7.4 1.9 gather_fusion.2
  9.4 3.7 collective-permute-start
  13.1 1.3 collective-permute-start.1
  14.4 3.3 copy.52
  17.7 2.0 gather_fusion.1
  19.7 1.7 copy.28
  21.4 0.1 copy.31
  21.5 0.1 reshape.133
  21.7 1.0 collective-permute-done.1
  22.7 0.2 pad_maximum_fusion.1
  22.9 3.0 gather_fusion.3
  26.0 9.6 %fusion.22 = bf16[32,4,128,128]{2,3,1,0:T(8,128)(2,1)} fusion(f32[32,128]{1,0:T(8,128)S(1)} %copy.30, f32[32,128,128]{1,2,0:T(8,128)} %copy.28, pred[4]{0:T(512)(128)(4,1)S(1)} %iota_compare_fusion.2, bf16[32,4,128,128]{3,2,1,0:T(8,128)(2,1)} %bitcast.110, bf16[32,4,128,128]{3,2,1,0:T(8,128)(2,1)} %param.8), kind=kOutput, calls=%fused_computation.31 | convolution fusion | flops 545259520 | bytes 14696452 | tf_op jit(solution)/shard_map/tkxz,tkzy->tkxy/dot_general | solution.py:65
  35.5 3.2 gather_fusion.4
  38.7 1.2 fusion.25
  39.9 3.6 collective-permute-start.2
  43.5 1.3 collective-permute-start.3
  44.8 0.1 reshape.106
  44.9 0.1 reshape.103
  45.0 0.1 reshape.108
  45.0 20.5 %collective-permute-done.2 = bf16[8,4,128,128]{2,3,1,0:T(8,128)(2,1)S(1)} collective-permute-done((bf16[8,4,128,128]{2,3,1,0:T(8,128)(2,1)}, bf16[8,4,128,128]{2,3,1,0:T(8,128)(2,1)S(1)}, u32[]{:S(2)}, u32[]{:S(2)}) %collective-permute-start.2) | collective-permute-done | bytes 1048608 | tf_op jit(solution)/shard_map/ppermute | solution.py:22
  65.6 3.9 collective-permute-done.3
  69.4 6.3 %pad_maximum_fusion = bf16[48,4,128,128]{2,3,1,0:T(8,128)(2,1)} fusion(bf16[8,4,128,128]{2,3,1,0:T(8,128)(2,1)S(1)} %collective-permute-done.3, bf16[8,4,128,128]{2,3,1,0:T(8,128)(2,1)S(1)} %collective-permute-done.2, bf16[32,4,128,128]{2,3,1,0:T(8,128)(2,1)} %fusion.22), kind=kLoop, calls=%fused_computation.32 | loop fusion | flops 6291456 | bytes 12582912 | tf_op jit(solution)/shard_map/concatenate | solution.py:74
  75.7 8.7 %copy.36 = bf16[48,4,128,128]{3,2,1,0:T(8,128)(2,1)} copy(bf16[48,4,128,128]{2,3,1,0:T(8,128)(2,1)} %pad_maximum_fusion) | data formatting | bytes 12582912
  84.4 325.7 %while.11 = (s32[]{:T(128)}, f32[6,128,1280]{2,0,1:T(8,128)}, s32[4,8,4]{1,0,2:T(4,128)S(1)}, bf16[4,8,4,128,128]{3,4,2,1,0:T(8,128)(2,1)}, s32[4,8,4]{1,0,2:T(4...) while((s32[]{:T(128)}, f32[6,128,1280]{2,0,1:T(8,128)}, ...), condition=%wide.region_1.2_spmd.clone, body=%wide.region_0.1_spmd.clone.sunk | while | flops 2511473152 | bytes 108536064 | solution.py:91
  84.4 0.1 copy.63
  84.7 5.8 %gather_fusion = bf16[32,4,128,128]{3,2,1,0:T(8,128)(2,1)} fusion(bf16[48,4,128,128]{3,2,1,0:T(8,128)(2,1)} %get-tuple-element.208, s32[1024]{0:T(1024)S(1)} %pad_clamp_fusion.4), kind=kCustom, calls=%fused_computation.clone.clone.1 | custom fusion | bytes 8388736 | tf_op jit(solution)/shard_map/while/body/eval_jaxpr/gather | solution.py:34
  90.5 7.0 %fusion.50 = f32[8,4,4,128,128]{4,3,2,1,0:T(8,128)} fusion(bf16[8,4,4,128,128]{4,3,2,1,0:T(8,128)(2,1)} %bitcast.104, bf16[4,8,4,128,128]{4,3,2,1,0:T(8,128)(2,1)} %get-tuple-element.209, s32[]{:T(128)S(6)} %copy.69), kind=kOutput, calls=%fused_computation.13.clone.1 | convolution fusion | flops 536870912 | bytes 13631492 | tf_op jit(solution)/shard_map/while/body/eval_jaxpr/tkxz,tkmzy->tkmxy/dot_general | solution.py:35
  97.5 9.2 %copy.64 = f32[8,16,128,128]{3,1,2,0:T(8,128)} copy(f32[8,16,128,128]{2,3,1,0:T(8,128)} %bitcast.103) | data formatting | bytes 16777216 | tf_op jit(solution)/shard_map/while/body/eval_jaxpr/reshape | solution.py:38
  106.7 9.8 %convert_bitcast_fusion.2 = bf16[8,128,10,128]{3,2,1,0:T(8,128)(2,1)} fusion(f32[8,16,128,128]{3,1,2,0:T(8,128)} %copy.64, s32[8,16]{1,0:T(8,128)S(1)} %copy.65), kind=kOutput, calls=%fused_computation.10.clone.1 | convolution fusion | flops 252970240 | bytes 11010560 | tf_op jit(solution)/shard_map/while/body/eval_jaxpr/tnc,tnxy->txcy/dot_general | solution.py:40
  116.5 6.8 %copy.66 = bf16[8,128,10,128]{1,3,2,0:T(8,128)(2,1)S(1)} copy(bf16[8,128,10,128]{3,2,1,0:T(8,128)(2,1)} %convert_bitcast_fusion.2) | data formatting | bytes 5242880 | tf_op jit(solution)/shard_map/while/body/eval_jaxpr/convert_element_type | solution.py:41
  123.3 11.1 %fusion.51 = f32[8,4,128,1280]{3,2,1,0:T(8,128)} fusion(bf16[8,128,1280,1]{1,2,3,0:T(8,128)(2,1)S(1)} %bitcast.105, bf16[4,8,4,128,128]{3,4,2,1,0:T(8,128)(2,1)} %get-tuple-element.206, s32[]{:T(128)S(6)} %copy.69), kind=kOutput, calls=%fused_computation.11.clone.1 | convolution fusion | flops 1342177280 | bytes 24641540 | tf_op jit(solution)/shard_map/while/body/eval_jaxpr/tmzx,tzc->tmxc/dot_general | solution.py:42
  134.4 30.3 %bitcast_add_fusion.2 = f32[6,128,1280]{2,0,1:T(8,128)} fusion(f32[6,128,1280]{2,0,1:T(8,128)} %get-tuple-element.194, f32[8,4,128,1280]{3,2,1,0:T(8,128)} %fusion.51, pred[]{:T(512)S(6)} %compare.6, s32[8,4]{0,1:T(4,128)S(1)} %bitcast.116), kind=kOutput, calls=%fused_computation.9.clone.1 | convolution fusion | flops 379453632 | bytes 28835968 | tf_op jit(solution)/shard_map/while/body/eval_jaxpr/tmr,tmxc->rxc/dot_general | solution.py:44
  164.9 5.8 %gather_fusion = bf16[32,4,128,128]{3,2,1,0:T(8,128)(2,1)} fusion(bf16[48,4,128,128]{3,2,1,0:T(8,128)(2,1)} %get-tuple-element.208, s32[1024]{0:T(1024)S(1)} %pad_clamp_fusion.4), kind=kCustom, calls=%fused_computation.clone.clone.1 | custom fusion | bytes 8388736 | tf_op jit(solution)/shard_map/while/body/eval_jaxpr/gather | solution.py:34
  170.7 7.0 %fusion.50 = f32[8,4,4,128,128]{4,3,2,1,0:T(8,128)} fusion(bf16[8,4,4,128,128]{4,3,2,1,0:T(8,128)(2,1)} %bitcast.104, bf16[4,8,4,128,128]{4,3,2,1,0:T(8,128)(2,1)} %get-tuple-element.209, s32[]{:T(128)S(6)} %copy.69), kind=kOutput, calls=%fused_computation.13.clone.1 | convolution fusion | flops 536870912 | bytes 13631492 | tf_op jit(solution)/shard_map/while/body/eval_jaxpr/tkxz,tkmzy->tkmxy/dot_general | solution.py:35
  177.8 9.2 %copy.64 = f32[8,16,128,128]{3,1,2,0:T(8,128)} copy(f32[8,16,128,128]{2,3,1,0:T(8,128)} %bitcast.103) | data formatting | bytes 16777216 | tf_op jit(solution)/shard_map/while/body/eval_jaxpr/reshape | solution.py:38
  187.0 9.8 %convert_bitcast_fusion.2 = bf16[8,128,10,128]{3,2,1,0:T(8,128)(2,1)} fusion(f32[8,16,128,128]{3,1,2,0:T(8,128)} %copy.64, s32[8,16]{1,0:T(8,128)S(1)} %copy.65), kind=kOutput, calls=%fused_computation.10.clone.1 | convolution fusion | flops 252970240 | bytes 11010560 | tf_op jit(solution)/shard_map/while/body/eval_jaxpr/tnc,tnxy->txcy/dot_general | solution.py:40
  196.7 6.8 %copy.66 = bf16[8,128,10,128]{1,3,2,0:T(8,128)(2,1)S(1)} copy(bf16[8,128,10,128]{3,2,1,0:T(8,128)(2,1)} %convert_bitcast_fusion.2) | data formatting | bytes 5242880 | tf_op jit(solution)/shard_map/while/body/eval_jaxpr/convert_element_type | solution.py:41
  203.5 11.1 %fusion.51 = f32[8,4,128,1280]{3,2,1,0:T(8,128)} fusion(bf16[8,128,1280,1]{1,2,3,0:T(8,128)(2,1)S(1)} %bitcast.105, bf16[4,8,4,128,128]{3,4,2,1,0:T(8,128)(2,1)} %get-tuple-element.206, s32[]{:T(128)S(6)} %copy.69), kind=kOutput, calls=%fused_computation.11.clone.1 | convolution fusion | flops 1342177280 | bytes 24641540 | tf_op jit(solution)/shard_map/while/body/eval_jaxpr/tmzx,tzc->tmxc/dot_general | solution.py:42
  214.6 31.8 %bitcast_add_fusion.2 = f32[6,128,1280]{2,0,1:T(8,128)} fusion(f32[6,128,1280]{2,0,1:T(8,128)} %get-tuple-element.194, f32[8,4,128,1280]{3,2,1,0:T(8,128)} %fusion.51, pred[]{:T(512)S(6)} %compare.6, s32[8,4]{0,1:T(4,128)S(1)} %bitcast.116), kind=kOutput, calls=%fused_computation.9.clone.1 | convolution fusion | flops 379453632 | bytes 28835968 | tf_op jit(solution)/shard_map/while/body/eval_jaxpr/tmr,tmxc->rxc/dot_general | solution.py:44
  246.7 5.8 %gather_fusion = bf16[32,4,128,128]{3,2,1,0:T(8,128)(2,1)} fusion(bf16[48,4,128,128]{3,2,1,0:T(8,128)(2,1)} %get-tuple-element.208, s32[1024]{0:T(1024)S(1)} %pad_clamp_fusion.4), kind=kCustom, calls=%fused_computation.clone.clone.1 | custom fusion | bytes 8388736 | tf_op jit(solution)/shard_map/while/body/eval_jaxpr/gather | solution.py:34
  252.6 7.0 %fusion.50 = f32[8,4,4,128,128]{4,3,2,1,0:T(8,128)} fusion(bf16[8,4,4,128,128]{4,3,2,1,0:T(8,128)(2,1)} %bitcast.104, bf16[4,8,4,128,128]{4,3,2,1,0:T(8,128)(2,1)} %get-tuple-element.209, s32[]{:T(128)S(6)} %copy.69), kind=kOutput, calls=%fused_computation.13.clone.1 | convolution fusion | flops 536870912 | bytes 13631492 | tf_op jit(solution)/shard_map/while/body/eval_jaxpr/tkxz,tkmzy->tkmxy/dot_general | solution.py:35
  259.6 9.2 %copy.64 = f32[8,16,128,128]{3,1,2,0:T(8,128)} copy(f32[8,16,128,128]{2,3,1,0:T(8,128)} %bitcast.103) | data formatting | bytes 16777216 | tf_op jit(solution)/shard_map/while/body/eval_jaxpr/reshape | solution.py:38
  268.8 9.8 %convert_bitcast_fusion.2 = bf16[8,128,10,128]{3,2,1,0:T(8,128)(2,1)} fusion(f32[8,16,128,128]{3,1,2,0:T(8,128)} %copy.64, s32[8,16]{1,0:T(8,128)S(1)} %copy.65), kind=kOutput, calls=%fused_computation.10.clone.1 | convolution fusion | flops 252970240 | bytes 11010560 | tf_op jit(solution)/shard_map/while/body/eval_jaxpr/tnc,tnxy->txcy/dot_general | solution.py:40
  278.6 6.8 %copy.66 = bf16[8,128,10,128]{1,3,2,0:T(8,128)(2,1)S(1)} copy(bf16[8,128,10,128]{3,2,1,0:T(8,128)(2,1)} %convert_bitcast_fusion.2) | data formatting | bytes 5242880 | tf_op jit(solution)/shard_map/while/body/eval_jaxpr/convert_element_type | solution.py:41
  285.4 11.1 %fusion.51 = f32[8,4,128,1280]{3,2,1,0:T(8,128)} fusion(bf16[8,128,1280,1]{1,2,3,0:T(8,128)(2,1)S(1)} %bitcast.105, bf16[4,8,4,128,128]{3,4,2,1,0:T(8,128)(2,1)} %get-tuple-element.206, s32[]{:T(128)S(6)} %copy.69), kind=kOutput, calls=%fused_computation.11.clone.1 | convolution fusion | flops 1342177280 | bytes 24641540 | tf_op jit(solution)/shard_map/while/body/eval_jaxpr/tmzx,tzc->tmxc/dot_general | solution.py:42
  296.4 31.8 %bitcast_add_fusion.2 = f32[6,128,1280]{2,0,1:T(8,128)} fusion(f32[6,128,1280]{2,0,1:T(8,128)} %get-tuple-element.194, f32[8,4,128,1280]{3,2,1,0:T(8,128)} %fusion.51, pred[]{:T(512)S(6)} %compare.6, s32[8,4]{0,1:T(4,128)S(1)} %bitcast.116), kind=kOutput, calls=%fused_computation.9.clone.1 | convolution fusion | flops 379453632 | bytes 28835968 | tf_op jit(solution)/shard_map/while/body/eval_jaxpr/tmr,tmxc->rxc/dot_general | solution.py:44
  328.5 5.8 %gather_fusion = bf16[32,4,128,128]{3,2,1,0:T(8,128)(2,1)} fusion(bf16[48,4,128,128]{3,2,1,0:T(8,128)(2,1)} %get-tuple-element.208, s32[1024]{0:T(1024)S(1)} %pad_clamp_fusion.4), kind=kCustom, calls=%fused_computation.clone.clone.1 | custom fusion | bytes 8388736 | tf_op jit(solution)/shard_map/while/body/eval_jaxpr/gather | solution.py:34
  334.4 7.0 %fusion.50 = f32[8,4,4,128,128]{4,3,2,1,0:T(8,128)} fusion(bf16[8,4,4,128,128]{4,3,2,1,0:T(8,128)(2,1)} %bitcast.104, bf16[4,8,4,128,128]{4,3,2,1,0:T(8,128)(2,1)} %get-tuple-element.209, s32[]{:T(128)S(6)} %copy.69), kind=kOutput, calls=%fused_computation.13.clone.1 | convolution fusion | flops 536870912 | bytes 13631492 | tf_op jit(solution)/shard_map/while/body/eval_jaxpr/tkxz,tkmzy->tkmxy/dot_general | solution.py:35
  341.4 9.2 %copy.64 = f32[8,16,128,128]{3,1,2,0:T(8,128)} copy(f32[8,16,128,128]{2,3,1,0:T(8,128)} %bitcast.103) | data formatting | bytes 16777216 | tf_op jit(solution)/shard_map/while/body/eval_jaxpr/reshape | solution.py:38
  350.6 9.8 %convert_bitcast_fusion.2 = bf16[8,128,10,128]{3,2,1,0:T(8,128)(2,1)} fusion(f32[8,16,128,128]{3,1,2,0:T(8,128)} %copy.64, s32[8,16]{1,0:T(8,128)S(1)} %copy.65), kind=kOutput, calls=%fused_computation.10.clone.1 | convolution fusion | flops 252970240 | bytes 11010560 | tf_op jit(solution)/shard_map/while/body/eval_jaxpr/tnc,tnxy->txcy/dot_general | solution.py:40
  360.4 6.8 %copy.66 = bf16[8,128,10,128]{1,3,2,0:T(8,128)(2,1)S(1)} copy(bf16[8,128,10,128]{3,2,1,0:T(8,128)(2,1)} %convert_bitcast_fusion.2) | data formatting | bytes 5242880 | tf_op jit(solution)/shard_map/while/body/eval_jaxpr/convert_element_type | solution.py:41
  367.2 11.1 %fusion.51 = f32[8,4,128,1280]{3,2,1,0:T(8,128)} fusion(bf16[8,128,1280,1]{1,2,3,0:T(8,128)(2,1)S(1)} %bitcast.105, bf16[4,8,4,128,128]{3,4,2,1,0:T(8,128)(2,1)} %get-tuple-element.206, s32[]{:T(128)S(6)} %copy.69), kind=kOutput, calls=%fused_computation.11.clone.1 | convolution fusion | flops 1342177280 | bytes 24641540 | tf_op jit(solution)/shard_map/while/body/eval_jaxpr/tmzx,tzc->tmxc/dot_general | solution.py:42
  378.3 31.8 %bitcast_add_fusion.2 = f32[6,128,1280]{2,0,1:T(8,128)} fusion(f32[6,128,1280]{2,0,1:T(8,128)} %get-tuple-element.194, f32[8,4,128,1280]{3,2,1,0:T(8,128)} %fusion.51, pred[]{:T(512)S(6)} %compare.6, s32[8,4]{0,1:T(4,128)S(1)} %bitcast.116), kind=kOutput, calls=%fused_computation.9.clone.1 | convolution fusion | flops 379453632 | bytes 28835968 | tf_op jit(solution)/shard_map/while/body/eval_jaxpr/tmr,tmxc->rxc/dot_general | solution.py:44
  410.1 7.9 %fusion.24 = (f32[2,128,1280]{2,0,1:T(2,128)S(1)}, f32[2,128,1280]{2,0,1:T(2,128)S(1)}, f32[2,128,1280]{2,0,1:T(2,128)S(1)}) fusion(f32[6,128,1280]{2,0,1:T(8,128)} %get-tuple-element.57), kind=kLoop, calls=%fused_computation.43 | loop fusion | bytes 7864320 | tf_op jit(solution)/shard_map/slice | solution.py:19
  418.0 0.1 copy.38
  418.1 0.1 copy.40
  418.2 1.3 collective-permute-start.5
  419.5 5.1 %collective-permute-start.4 = (f32[1,256,1280]{2,1,0:T(8,128)S(1)}, f32[1,256,1280]{2,1,0:T(8,128)S(1)}, u32[]{:S(2)}, u32[]{:S(2)}) collective-permute-start(f32[1,256,1280]{2,1,0:T(8,128)S(1)} %bitcast.111), channel_id=1, source_target_pairs={{0,8},{8,16},{16,24},{24,32},{32,40},{40,48},{48,56},{56,64},{64,7... | collective-permute-start | bytes 3932168 | tf_op jit(solution)/shard_map/ppermute | solution.py:22
  424.6 0.1 copy.39
  424.7 24.5 %collective-permute-done.5 = f32[1,256,1280]{2,1,0:T(8,128)S(1)} collective-permute-done((f32[1,256,1280]{2,1,0:T(8,128)S(1)}, f32[1,256,1280]{2,1,0:T(8,128)S(1)}, u32[]{:S(2)}, u32[]{:S(2)}) %collective-permute-start.5) | collective-permute-done | bytes 1310752 | tf_op jit(solution)/shard_map/ppermute | solution.py:24
  449.2 1.2 collective-permute-done.4
  450.4 1.5 pad_add_fusion
  451.9 41.9 %reduce-scatter.2.cloned.1.call-done = f32[32,1792]{1,0:T(8,128)} async-done(((f32[256,1792]{1,0:T(8,128)}), f32[32,1792]{1,0:T(8,128)}) %reduce-scatter.2.cloned.1.call-update) | async-done | bytes 229392 | tf_op jit(solution)/shard_map/reduce_scatter | solution.py:95
  (52 shorter events, 1.2 us)
Async XLA Ops:
  6.5 7.9 %slice-start = ((bf16[32,4,128,128]{3,2,1,0:T(8,128)(2,1)}), bf16[32,1,128,128]{3,2,1,0:T(8,128)(2,1)S(1)}, s32[]{:S(2)}) async-start(bf16[32,4,128,128]{3,2,1,0:T(8,128)(2,1)} %param.8), calls=%async_computation.2 | async-start | bytes 2097152 | tf_op jit(solution)/shard_map/slice | solution.py:66
  6.5 487.2 %reduce-scatter.2.cloned.1.call-start = ((), (), s32[]{:S(2)}) async-start(), calls=%async_computation.1 | async-start | bytes 2064384 | tf_op jit(solution)/shard_map/reduce_scatter | solution.py:95
  9.3 10.4 %copy-start.3 = (s32[32,4]{0,1:T(4,128)S(1)}, s32[32,4]{0,1:T(4,128)}, u32[]{:S(2)}) copy-start(s32[32,4]{0,1:T(4,128)} %param.9) | copy-start | bytes 1540
  9.3 10.4 %copy-start = (bf16[32,128,128]{2,1,0:T(8,128)(2,1)S(1)}, bf16[32,128,128]{2,1,0:T(8,128)(2,1)}, u32[]{:S(2)}) copy-start(bf16[32,128,128]{2,1,0:T(8,128)(2,1)} %param.11) | copy-start | bytes 3145732
  9.4 12.3 %collective-permute-start = (bf16[8,128,128]{2,1,0:T(8,128)(2,1)S(1)}, bf16[8,128,128]{2,1,0:T(8,128)(2,1)S(1)}, u32[]{:S(2)}, u32[]{:S(2)}) collective-permute-start(bf16[8,128,128]{2,1,0:T(8,128)(2,1)S(1)} %get-tuple-element.128), channel_id=1, source_target_pairs={{0,8},{8,16},{16,24},{24,32},{32,40},{40,48},{48,56},{56,64},{64,7... | collective-permute-start | bytes 786440 | tf_op jit(solution)/shard_map/ppermute | solution.py:22
  13.1 9.7 %collective-permute-start.1 = (bf16[8,128,128]{2,1,0:T(8,128)(2,1)S(1)}, bf16[8,128,128]{2,1,0:T(8,128)(2,1)S(1)}, u32[]{:S(2)}, u32[]{:S(2)}) collective-permute-start(bf16[8,128,128]{2,1,0:T(8,128)(2,1)S(1)} %get-tuple-element.129), channel_id=1, source_target_pairs={{8,0},{16,8},{24,16},{32,24},{40,32},{48,40},{56,48},{64,56},{72,6... | collective-permute-start | bytes 786440 | tf_op jit(solution)/shard_map/ppermute | solution.py:24
  17.7 5.0 %copy-start.1 = (bf16[32,128,128]{2,1,0:T(8,128)(2,1)S(1)}, bf16[32,128,128]{2,1,0:T(8,128)(2,1)}, u32[]{:S(2)}) copy-start(bf16[32,128,128]{2,1,0:T(8,128)(2,1)} %param.11) | copy-start | bytes 3145732
  35.5 9.3 %copy-start.4 = (s32[32,4]{0,1:T(4,128)S(1)}, s32[32,4]{0,1:T(4,128)}, u32[]{:S(2)}) copy-start(s32[32,4]{0,1:T(4,128)} %param.12) | copy-start | bytes 1540
  35.5 9.4 %copy-start.2 = (s32[32,4,4]{0,2,1:T(4,128)S(1)}, s32[32,4,4]{0,2,1:T(4,128)}, u32[]{:S(2)}) copy-start(s32[32,4,4]{0,2,1:T(4,128)} %param.13) | copy-start | bytes 6148
  39.9 25.7 %collective-permute-start.2 = (bf16[8,4,128,128]{2,3,1,0:T(8,128)(2,1)}, bf16[8,4,128,128]{2,3,1,0:T(8,128)(2,1)S(1)}, u32[]{:S(2)}, u32[]{:S(2)}) collective-permute-start(bf16[8,4,128,128]{2,3,1,0:T(8,128)(2,1)} %get-tuple-element.126), channel_id=1, source_target_pairs={{0,8},{8,16},{16,24},{24,32},{32,40},{40,48},{48,56},{56,64},{64,7... | collective-permute-start | bytes 3145736 | tf_op jit(solution)/shard_map/ppermute | solution.py:22
  43.5 26.0 %collective-permute-start.3 = (bf16[8,4,128,128]{2,3,1,0:T(8,128)(2,1)S(1)}, bf16[8,4,128,128]{2,3,1,0:T(8,128)(2,1)S(1)}, u32[]{:S(2)}, u32[]{:S(2)}) collective-permute-start(bf16[8,4,128,128]{2,3,1,0:T(8,128)(2,1)S(1)} %get-tuple-element.127), channel_id=1, source_target_pairs={{8,0},{16,8},{24,16},{32,24},{40,32},{48,40},{56,48},{64,56},{72,6... | collective-permute-start | bytes 3145736 | tf_op jit(solution)/shard_map/ppermute | solution.py:24
  418.2 31.1 %collective-permute-start.5 = (f32[1,256,1280]{2,1,0:T(8,128)S(1)}, f32[1,256,1280]{2,1,0:T(8,128)S(1)}, u32[]{:S(2)}, u32[]{:S(2)}) collective-permute-start(f32[1,256,1280]{2,1,0:T(8,128)S(1)} %bitcast.112), channel_id=1, source_target_pairs={{8,0},{16,8},{24,16},{32,24},{40,32},{48,40},{56,48},{64,56},{72,6... | collective-permute-start | bytes 3932168 | tf_op jit(solution)/shard_map/ppermute | solution.py:24
  419.5 30.9 %collective-permute-start.4 = (f32[1,256,1280]{2,1,0:T(8,128)S(1)}, f32[1,256,1280]{2,1,0:T(8,128)S(1)}, u32[]{:S(2)}, u32[]{:S(2)}) collective-permute-start(f32[1,256,1280]{2,1,0:T(8,128)S(1)} %bitcast.111), channel_id=1, source_target_pairs={{0,8},{8,16},{16,24},{24,32},{32,40},{40,48},{48,56},{56,64},{64,7... | collective-permute-start | bytes 3932168 | tf_op jit(solution)/shard_map/ppermute | solution.py:22
Sparse Core Ops, SparseCore 0:
  452.0 41.7 reduce-scatter.1
where the time goes:
time: 502 us; the launch traced here: 501 us
  matrix products  247 us (49%)
  local copies, waits for them, and re-layouts  123 us (25%)
  waiting for transfers between devices  93.1 us (19%)
  starting transfers between devices  16.3 us (3%)
  between operations  13.6 us (3%)
  other arithmetic  8.06 us (2%)
    dot_general x4, matrix products, block_terms(): jnp.einsum('tmr,tmxc->rxc', pick_slots, weighted, precision=lax.Precision...  126 us
    dot_general x4, matrix products, block_terms(): jnp.einsum('tmzx,tzc->tmxc', blk_smooth, placed, preferred_element_type=j...  44.3 us
    reduce_scatter x1, waiting for transfers between devices, on_device(): return lax.psum_scatter(coarse_band, 'sub', scatter_dimension=0, tiled=True)  41.9 us
    dot_general x4, matrix products, block_terms(): jnp.einsum('tnc,tnxy->txcy', pick_cols, products, precision=lax.Precision...  39.1 us
    reshape x4, local copies, waits for them, and re-layouts, block_terms(): products = products.reshape(blk_count, K * K, B, B)  36.7 us
    ppermute x3, waiting for transfers between devices, extended(): lax.ppermute(head, axis, [((i + 1) % count, i) for i in range(ends)])  29.5 us
    dot_general x4, matrix products, block_terms(): jnp.einsum('tkxz,tkmzy->tkmxy', blk_tiles, fetched, preferred_element_typ...  28.2 us
    convert_element_type x4, local copies, waits for them, and re-layouts, block_terms(): placed = placed.reshape(blk_count, B, 5 * NCG * B).astype(jnp.bfloat16)  27.1 us
  transfers between devices with their start and end apart: 7, of which 6 were waited for; matrix products, arithmetic and copies ran while one was open for 2% of the time, Pallas kernels for 0%

commit v1 on v0

v1 whole, which is shorter than its diff:
```python
import jax
import jax.numpy as jnp
from jax import lax
from jax.experimental import pallas as pl
from jax.experimental.pallas import tpu as pltpu
from jax.sharding import PartitionSpec as P

B = 128
K = 4
TR = 32
NCG = 2
GD = 8
G = NCG * B
OMEGA = 0.6
F32 = jnp.float32
BF16 = jnp.bfloat16
MESH = pl.DeviceIdType.MESH


def smooth_tiles(a_v, t_ext, cols_ref, row, eye):
    diagonal = jnp.sum(jnp.where(eye, a_v[row, 0].astype(F32), 0.0), axis=1, keepdims=True)
    weight = OMEGA * (1.0 / diagonal)
    tiles = []
    for m in range(K):
        product = jnp.dot(a_v[row, m], t_ext[cols_ref[row, m]], preferred_element_type=F32)
        value = weight * product
        value = t_ext[row].astype(F32) - value if m == 0 else -value
        tiles.append(value.astype(BF16))
    return tiles


def slot_tile(tiles, factor, slot):
    total = None
    for m in range(K):
        if m == 0 and slot // NCG != 1:
            continue
        term = tiles[m] * factor(m, slot)
        total = term if total is None else total + term
    return total


def kernel(
    a_hbm, cols_ref, lists_ref, t_hbm, slots_ref, out_ref,
    a_v, t_own, t_ext, t_send, s_send, s_halo, pc_send, pc_halo,
    p_all, p_t, ap, part, core_in, q, x_in, x_fwd, y_in,
    load_sem, t_ssem, t_rsem, s_ssem, s_rsem, pc_ssem, pc_rsem,
    c_ssem, c_rsem, x_ssem, x_rsem, y_ssem, y_rsem,
):
    dom, sub = lax.axis_index("dom"), lax.axis_index("sub")
    n_dom = lax.axis_size("dom")
    up, down = lax.rem(dom + 1, n_dom), lax.rem(dom + n_dom - 1, n_dom)
    x, core = sub // 2, lax.rem(sub, 2)
    xa = x + 1 - 2 * lax.rem(x, 2)
    xb = 3 - x
    xo = lax.rem(x + 2, 4)
    to_up, to_down = (up, sub), (down, sub)
    to_core = (dom, 2 * x + 1 - core)
    to_a, to_b = (dom, 2 * xa + core), (dom, 2 * xb + core)

    load_own = pltpu.make_async_copy(t_hbm, t_own, load_sem.at[0])
    load_ext = pltpu.make_async_copy(t_hbm, t_ext.at[pl.ds(0, TR)], load_sem.at[1])
    load_a = pltpu.make_async_copy(a_hbm, a_v, load_sem.at[2])
    load_own.start()
    load_a.start()
    load_ext.start()

    barrier = pltpu.get_barrier_semaphore()
    for device in (to_up, to_down, to_core, to_a, to_b):
        pl.semaphore_signal(barrier, inc=1, device_id=device, device_id_type=MESH)

    for side in range(2):
        for j in range(GD):
            row = lists_ref[side, j]
            for m in range(K):
                pc_send[side, m, j : j + 1, :] = jnp.full((1, B), slots_ref[row, m], jnp.int32)

    def remote(src, dst, ssem, rsem, device):
        return pltpu.make_async_remote_copy(
            src_ref=src, dst_ref=dst, send_sem=ssem, recv_sem=rsem,
            device_id=device, device_id_type=MESH,
        )

    load_own.wait()

    def gather_row(j, carry):
        for side in range(2):
            t_send[side, j] = t_own[lists_ref[side, j]]
        return carry

    lax.fori_loop(0, GD, gather_row, 0)
    pl.semaphore_wait(barrier, 5)

    t_up = remote(t_send.at[1], t_ext.at[pl.ds(TR, GD)], t_ssem.at[0], t_rsem.at[0], to_up)
    t_down = remote(t_send.at[0], t_ext.at[pl.ds(TR + GD, GD)], t_ssem.at[1], t_rsem.at[1], to_down)
    t_up.start()
    t_down.start()
    pc_up = remote(pc_send.at[1], pc_halo.at[0], pc_ssem.at[0], pc_rsem.at[0], to_up)
    pc_down = remote(pc_send.at[0], pc_halo.at[1], pc_ssem.at[1], pc_rsem.at[1], to_down)
    pc_up.start()
    pc_down.start()

    empty = jnp.zeros((B, G), BF16)

    def clear(first, groups):
        def body(j, carry):
            for g in groups:
                p_all[first + j, g] = empty
            return carry

        return body

    lax.fori_loop(0, TR, clear(0, (0, 4)), 0)
    lax.fori_loop(0, GD, clear(TR, (3, 4)), 0)
    lax.fori_loop(0, GD, clear(TR + GD, (0, 1)), 0)

    load_a.wait()
    load_ext.wait()
    t_up.wait_recv()
    t_down.wait_recv()

    eye = lax.broadcasted_iota(jnp.int32, (B, B), 0) == lax.broadcasted_iota(jnp.int32, (B, B), 1)

    def send_row(j, carry):
        for side in range(2):
            tiles = smooth_tiles(a_v, t_ext, cols_ref, lists_ref[side, j], eye)
            for m in range(K):
                s_send[side, j, m] = tiles[m]
            region = GD * (1 - side)
            remote(
                s_send.at[side, j], s_halo.at[region + j], s_ssem.at[side], s_rsem.at[side],
                to_up if side == 1 else to_down,
            ).start()
        return carry

    lax.fori_loop(0, GD, send_row, 0)

    def own_row(row, carry):
        tiles = smooth_tiles(a_v, t_ext, cols_ref, row, eye)
        slots = [slots_ref[row, m] for m in range(K)]

        def factor(m, slot):
            return jnp.full((B, B), jnp.where(slots[m] == slot, 1.0, 0.0), F32).astype(BF16)

        lanes = pl.ds(pl.multiple_of(row * B, B), B)
        for slot in range(3 * NCG):
            g, h = slot // NCG, slot % NCG
            tile = slot_tile(tiles, factor, slot)
            p_all[row, g + 1, :, h * B : (h + 1) * B] = tile
            turned = tile.T
            for quarter in range(4):
                a, c = quarter // 2, quarter % 2
                first = c * 96 + g * 32
                p_t[2 * h + a, first : first + 32, lanes] = turned[quarter * 32 : quarter * 32 + 32]
        return carry

    lax.fori_loop(0, TR, own_row, 0)

    pc_up.wait_recv()
    pc_down.wait_recv()
    s_up = remote(s_send.at[1], s_halo.at[pl.ds(0, GD)], s_ssem.at[1], s_rsem.at[1], to_up)
    s_down = remote(s_send.at[0], s_halo.at[pl.ds(GD, GD)], s_ssem.at[0], s_rsem.at[0], to_down)
    s_up.wait_recv()
    s_down.wait_recv()

    def halo_rows(region):
        def body(j, carry):
            tiles = [s_halo[region * GD + j, m] for m in range(K)]
            lines = [pc_halo[region, m, pl.ds(j, 1), :] for m in range(K)]

            def factor(m, slot):
                ones = jnp.where(lines[m] == slot, 1.0, 0.0)
                block = jnp.broadcast_to(ones, (16, B)).astype(BF16)
                return jnp.concatenate([block] * (B // 16), axis=0)

            for slot in range(3 * NCG):
                g, h = slot // NCG, slot % NCG
                p_all[TR + region * GD + j, g + 2 * region, :, h * B : (h + 1) * B] = slot_tile(
                    tiles, factor, slot
                )
            return carry

        return body

    for region in range(2):
        lax.fori_loop(0, GD, halo_rows(region), 0)

    def place_row(row, carry):
        cols = [cols_ref[row, k] for k in range(K)]
        left = jnp.concatenate([a_v[row, k] for k in range(K)], axis=1)
        rows = pl.ds(pl.multiple_of(row * B, B), B)
        for g in range(5):
            first = 0 if 1 <= g <= 3 else 1
            right = jnp.concatenate([p_all[cols[k], g] for k in range(first, K)], axis=0)
            value = jnp.dot(left[:, first * B :], right, preferred_element_type=F32)
            ap[g, rows, :] = value.astype(BF16)
        return carry

    lax.fori_loop(0, TR, place_row, 0)

    def block_product(step, target):
        def body(n, carry):
            value = jnp.dot(p_t[target], ap[n], preferred_element_type=F32)
            lanes = pl.ds(pl.multiple_of(n * G, G), G)
            part[step, 0, :, lanes] = value[:96]
            part[step, 1, :, lanes] = value[96:]
            return carry

        lax.fori_loop(0, 5, body, 0)

    HALF = 48
    core_copies, x_copies = [], []
    targets = (xo, xa, xb, x)

    def core_sum(step):
        core_copies[step].wait_recv()
        q[step] = part[step, core] + core_in[step]

    def x_send(src, index, device):
        copy = remote(src, x_in.at[index], x_ssem.at[index], x_rsem.at[index], device)
        copy.start()
        x_copies.append(copy)

    def x_wait(index):
        x_copies[index].wait_recv()

    def finish(step):
        core_sum(step)
        if step == 0:
            x_send(q.at[0, pl.ds(0, HALF)], 0, to_a)
            x_send(q.at[0, pl.ds(HALF, HALF)], 1, to_b)
        elif step == 1:
            x_send(q.at[1, pl.ds(0, HALF)], 2, to_a)
            x_wait(1)
            x_fwd[1] = q[1, HALF:, :] + x_in[1]
        elif step == 2:
            x_send(q.at[2, pl.ds(HALF, HALF)], 3, to_b)
            x_wait(0)
            x_fwd[0] = q[2, :HALF, :] + x_in[0]
            x_send(x_fwd.at[1], 4, to_a)
            x_send(x_fwd.at[0], 5, to_b)

    for step in range(4):
        block_product(step, targets[step])
        copy = remote(
            part.at[step, 1 - core], core_in.at[step], c_ssem.at[step], c_rsem.at[step], to_core
        )
        copy.start()
        core_copies.append(copy)
        if step >= 1:
            finish(step - 1)
    core_sum(3)
    x_wait(2)
    x_wait(5)
    q[3, :HALF, :] = q[3, :HALF, :] + (x_in[2] + x_in[5])
    y_down = remote(q.at[3, pl.ds(0, 32)], y_in.at[1], y_ssem.at[1], y_rsem.at[1], to_down)
    y_down.start()
    x_wait(3)
    x_wait(4)
    q[3, HALF:, :] = q[3, HALF:, :] + (x_in[3] + x_in[4])
    y_up = remote(q.at[3, pl.ds(64, 32)], y_in.at[0], y_ssem.at[0], y_rsem.at[0], to_up)
    y_up.start()
    out_ref[:, :G] = jnp.zeros((32, G), F32)
    out_ref[:, G : 6 * G] = q[3, 32:64, :]
    out_ref[:, 6 * G :] = jnp.zeros((32, G), F32)
    y_up.wait_recv()
    y_down.wait_recv()

    @pl.when(dom > 0)
    def _():
        out_ref[:, : 5 * G] = out_ref[:, : 5 * G] + y_in[0]

    @pl.when(dom < n_dom - 1)
    def _():
        out_ref[:, 2 * G :] = out_ref[:, 2 * G :] + y_in[1]

    for copy in [t_up, t_down, pc_up, pc_down, s_up, s_down, y_up, y_down] + core_copies + x_copies:
        copy.wait_send()


def on_device(a_vals, a_cols, send_rows, tentative, p_cols, ap_cols):
    hbm = pl.BlockSpec(memory_space=pl.ANY)
    smem = pl.BlockSpec(memory_space=pltpu.SMEM)
    dma = pltpu.SemaphoreType.DMA
    return pl.pallas_call(
        kernel,
        out_shape=jax.ShapeDtypeStruct((32, 7 * G), F32),
        in_specs=[hbm, smem, smem, hbm, smem],
        out_specs=pl.BlockSpec(memory_space=pltpu.VMEM),
        scratch_shapes=[
            pltpu.VMEM((TR, K, B, B), BF16),
            pltpu.VMEM((TR, B, B), BF16),
            pltpu.VMEM((TR + 2 * GD, B, B), BF16),
            pltpu.VMEM((2, GD, B, B), BF16),
            pltpu.VMEM((2, GD, K, B, B), BF16),
            pltpu.VMEM((2 * GD, K, B, B), BF16),
            pltpu.VMEM((2, K, GD, B), jnp.int32),
            pltpu.VMEM((2, K, GD, B), jnp.int32),
            pltpu.VMEM((TR + 2 * GD, 5, B, G), BF16),
            pltpu.VMEM((4, 192, TR * B), BF16),
            pltpu.VMEM((5, TR * B, G), BF16),
            pltpu.VMEM((4, 2, 96, 5 * G), F32),
            pltpu.VMEM((4, 96, 5 * G), F32),
            pltpu.VMEM((4, 96, 5 * G), F32),
            pltpu.VMEM((6, 48, 5 * G), F32),
            pltpu.VMEM((2, 48, 5 * G), F32),
            pltpu.VMEM((2, 32, 5 * G), F32),
            dma((3,)),
            dma((2,)), dma((2,)), dma((2,)), dma((2,)), dma((2,)), dma((2,)),
            dma((4,)), dma((4,)), dma((6,)), dma((6,)), dma((2,)), dma((2,)),
        ],
        compiler_params=pltpu.CompilerParams(
            collective_id=0, has_side_effects=True, vmem_limit_bytes=60 * 1024 * 1024
        ),
        cost_estimate=pl.CostEstimate(flops=16_000_000_000, bytes_accessed=8_000_000, transcendentals=0),
    )(a_vals, a_cols, send_rows.reshape(2, GD), tentative, p_cols)


def solution(mesh):
    placed = (
        P(("dom", "sub"), None, None, None),
        P(("dom", "sub"), None),
        P(("dom", "sub"), None, None),
        P(("dom", "sub"), None, None),
        P(("dom", "sub"), None),
        P(("dom", "sub"), None, None),
    )
    return jax.shard_map(
        on_device, mesh=mesh, in_specs=placed, out_specs=P(("dom", "sub"), None), check_vma=False
    )
```

time: 502 us -> 92.6 us (0.18)
  matrix products: 247 us -> 0 us
  local copies, waits for them, and re-layouts: 123 us -> 4.37 us
  waiting for transfers between devices: 93.1 us -> 0 us
  Pallas kernels: 0 us -> 88 us
  starting transfers between devices: 16.3 us -> 0 us
  between operations: 13.6 us -> 0.01 us
  other arithmetic: 8.06 us -> 0 us
    dot_general x17 -> x0, matrix products: 247 us -> none  [the longest x4 126 us: block_terms(): jnp.einsum('tmr,tmxc->rxc', pick_slots, weighted, precision=lax.Precision...]
    pallas_call x0 -> x1, Pallas kernels: none -> 88 us  [on_device(): pl.pallas_call(kernel, out_shape=jax.ShapeDtypeStruct((32, 7 * G), F32),...]
    ppermute x6 -> x0, waiting for transfers between devices: 51.2 us -> none  [the longest x3 29.5 us: extended(): lax.ppermute(head, axis, [((i + 1) % count, i) for i in range(ends)])]
    reduce_scatter x1 -> x0, waiting for transfers between devices: 41.9 us -> none  [on_device(): return lax.psum_scatter(coarse_band, 'sub', scatter_dimension=0, tiled=True)]
    reshape x8 -> x0, local copies, waits for them, and re-layouts: 37.8 us -> none  [the longest x4 36.7 us: block_terms(): products = products.reshape(blk_count, K * K, B, B)]
    gather x8 -> x0, local copies, waits for them, and re-layouts: 33.4 us -> none  [the longest x4 23.3 us: block_terms(): fetched = ext_smooth[blk_cols]]
    convert_element_type x5 -> x0, local copies, waits for them, and re-layouts: 28.8 us -> none  [the longest x4 27.1 us: block_terms(): placed = placed.reshape(blk_count, B, 5 * NCG * B).astype(jnp.bfloat16)]
    ppermute x6 -> x0, starting transfers between devices: 16.3 us -> none  [the longest x3 12.4 us: extended(): lax.ppermute(tail, axis, [(i, (i + 1) % count) for i in range(ends)])]
  transfers between devices with their start and end apart: 7 -> 0, of which waited for: 6 -> 0; matrix products, arithmetic and copies ran while one was open for 2% -> 0% of each run, Pallas kernels for 0% -> 0%
where the time goes in v1:
time: 92.6 us; the launch traced here: 92.4 us
  Pallas kernels  88 us (95%)
  local copies, waits for them, and re-layouts  4.37 us (5%)
    pallas_call x1, Pallas kernels, on_device(): pl.pallas_call(kernel, out_shape=jax.ShapeDtypeStruct((32, 7 * G), F32),...  88 us
    unnamed x3, local copies, waits for them, and re-layouts  4.37 us

profile of v1, /device:TPU:0, one launch (start us, length us, event | category | flops | bytes accessed | tf_op | source)
XLA Modules:
  0.0 92.4 jit_solution(16766824862383942702)
XLA Ops:
  0.0 1.4 %copy.6.cols_ref = s32[32,4]{1,0:T(8,128)} copy(s32[32,4]{0,1:T(4,128)} %param.7) | data formatting | bytes 1024 | tf_op args[1]
  1.4 1.4 %copy.7.slots_ref = s32[32,4]{1,0:T(8,128)} copy(s32[32,4]{0,1:T(4,128)} %param.10) | data formatting | bytes 1024 | tf_op args[4]
  2.7 88.0 %shard_map.55 = f32[32,1792]{1,0:T(8,128)} custom-call(bf16[32,4,128,128]{3,2,1,0:T(8,128)(2,1)} %a_hbm.1, s32[32,4]{1,0:T(8,128)} %copy.6.cols_ref, s32[2,8]{1,0:T(2,128)} %bitcast.1, bf16[32,128,128]{2,1,0:T(8,128)(2,1)} %t_hbm.1, s32[32,4]{1,0:T(8,128)} %copy.7.slots_ref), custom_call_target="tpu_custom_call" | custom-call | flops 16000000000 | bytes 8000000 | tf_op jit(solution)/shard_map/pallas_call | solution.py:284
  90.7 1.6 %copy.9 = f32[32,1792]{1,0:T(8,128)} copy(f32[32,1792]{1,0:T(8,128)} %shard_map.55) | data formatting | bytes 458752

commit v2 on v1

v2 whole, which is shorter than its diff:
```python
import jax
import jax.numpy as jnp
from jax import lax
from jax.experimental import pallas as pl
from jax.experimental.pallas import tpu as pltpu
from jax.sharding import PartitionSpec as P

B = 128
K = 4
TR = 32
NCG = 2
GD = 8
G = NCG * B
HALF = 48
OMEGA = 0.6
F32 = jnp.float32
BF16 = jnp.bfloat16
MESH = pl.DeviceIdType.MESH


def row_weight(a_v, row, eye):
    diagonal = jnp.sum(jnp.where(eye, a_v[row, 0].astype(F32), 0.0), axis=1, keepdims=True)
    return OMEGA * (1.0 / diagonal)


def smooth_tiles(a_v, t_ext, cols_ref, row, eye, first):
    weight = row_weight(a_v, row, eye)
    tiles = []
    for m in range(first, K):
        product = jnp.dot(a_v[row, m], t_ext[cols_ref[m, row]], preferred_element_type=F32)
        value = weight * product
        value = t_ext[row].astype(F32) - value if m == 0 else -value
        tiles.append(value.astype(BF16))
    return tiles


def slot_tile(tiles, factor, slot):
    total = None
    for m in range(K):
        if m == 0 and slot // NCG != 1:
            continue
        term = tiles[m] * factor(m, slot)
        total = term if total is None else total + term
    return total


def kernel(
    a_hbm, cols_ref, lists_ref, t_hbm, slots_ref, out_ref,
    a_v, t_own, t_ext, t_send, s0_send, s0_halo, s_send, s_halo, pc_send, pc_halo,
    p_all, p_t, ap, part, core_in, q, x1_in, x2_out, x2_in, fin, y_in,
    load_sem, t_ssem, t_rsem, s0_ssem, s0_rsem, s_ssem, s_rsem, pc_ssem, pc_rsem,
    c_ssem, c_rsem, x1_ssem, x1_rsem, x2_ssem, x2_rsem, y_ssem, y_rsem,
):
    dom, sub = lax.axis_index("dom"), lax.axis_index("sub")
    n_dom = lax.axis_size("dom")
    up, down = lax.rem(dom + 1, n_dom), lax.rem(dom + n_dom - 1, n_dom)
    x, core = sub // 2, lax.rem(sub, 2)
    xa = x + 1 - 2 * lax.rem(x, 2)
    xb = 3 - x
    xo = lax.rem(x + 2, 4)
    to_up, to_down = (up, sub), (down, sub)
    to_core = (dom, 2 * x + 1 - core)
    to_a, to_b = (dom, 2 * xa + core), (dom, 2 * xb + core)

    load_own = pltpu.make_async_copy(t_hbm, t_own, load_sem.at[0])
    load_ext = pltpu.make_async_copy(t_hbm, t_ext.at[pl.ds(0, TR)], load_sem.at[1])
    load_a = pltpu.make_async_copy(a_hbm, a_v, load_sem.at[2])
    load_own.start()
    load_a.start()
    load_ext.start()

    barrier = pltpu.get_barrier_semaphore()
    for device in (to_up, to_down, to_core, to_a, to_b):
        pl.semaphore_signal(barrier, inc=1, device_id=device, device_id_type=MESH)

    def remote(src, dst, ssem, rsem, device):
        return pltpu.make_async_remote_copy(
            src_ref=src, dst_ref=dst, send_sem=ssem, recv_sem=rsem,
            device_id=device, device_id_type=MESH,
        )

    eye = lax.broadcasted_iota(jnp.int32, (B, B), 0) == lax.broadcasted_iota(jnp.int32, (B, B), 1)

    load_own.wait()

    def gather_row(j, carry):
        for side in range(2):
            t_send[side, j] = t_own[lists_ref[side, j]]
        return carry

    lax.fori_loop(0, GD, gather_row, 0, unroll=4)

    for side in range(2):
        for j in range(GD):
            row = lists_ref[side, j]
            for m in range(K):
                pc_send[side, m, j : j + 1, :] = jnp.full((1, B), slots_ref[m, row], jnp.int32)

    load_a.wait()

    def first_tile(j, carry):
        for side in range(2):
            row = lists_ref[side, j]
            product = jnp.dot(a_v[row, 0], t_own[row], preferred_element_type=F32)
            value = t_own[row].astype(F32) - row_weight(a_v, row, eye) * product
            s0_send[side, j] = value.astype(BF16)
        return carry

    lax.fori_loop(0, GD, first_tile, 0, unroll=4)
    pl.semaphore_wait(barrier, 5)

    early = []
    for send, halo, ssem, rsem in (
        (t_send, None, t_ssem, t_rsem), (pc_send, pc_halo, pc_ssem, pc_rsem), (s0_send, s0_halo, s0_ssem, s0_rsem),
    ):
        for region, device in ((0, to_up), (1, to_down)):
            target = t_ext.at[pl.ds(TR + GD * region, GD)] if halo is None else halo.at[region]
            early.append(remote(send.at[1 - region], target, ssem.at[region], rsem.at[region], device))
            early[-1].start()

    empty = jnp.zeros((B, G), BF16)

    def clear(first, groups):
        def body(j, carry):
            for g in groups:
                p_all[first + j, g] = empty
            return carry

        return body

    lax.fori_loop(0, TR, clear(0, (0, 4)), 0)
    lax.fori_loop(0, GD, clear(TR, (3, 4)), 0)
    lax.fori_loop(0, GD, clear(TR + GD, (0, 1)), 0)

    load_ext.wait()
    early[0].wait_recv()
    early[1].wait_recv()

    def send_row(j, carry):
        for side in range(2):
            tiles = smooth_tiles(a_v, t_ext, cols_ref, lists_ref[side, j], eye, 1)
            for m in range(1, K):
                s_send[side, j, m - 1] = tiles[m - 1]
            remote(
                s_send.at[side, j], s_halo.at[1 - side, j], s_ssem.at[side], s_rsem.at[side],
                to_up if side == 1 else to_down,
            ).start()
        return carry

    lax.fori_loop(0, GD, send_row, 0, unroll=2)

    def order(target, one, two):
        return jnp.where(target == xo, 0, jnp.where(target == one, 1, jnp.where(target == two, 2, 3)))

    place_of = [[order(t, xa, xb) for t in range(4)], [order(t, xb, xa) for t in range(4)]]

    def own_row(row, carry):
        tiles = smooth_tiles(a_v, t_ext, cols_ref, row, eye, 0)
        slots = [slots_ref[m, row] for m in range(K)]

        def factor(m, slot):
            return jnp.full((B, B), jnp.where(slots[m] == slot, 1.0, 0.0), F32).astype(BF16)

        lanes = pl.ds(pl.multiple_of(row * B, B), B)
        for slot in range(3 * NCG):
            g, h = slot // NCG, slot % NCG
            tile = slot_tile(tiles, factor, slot)
            p_all[row, g + 1, :, h * B : (h + 1) * B] = tile
            turned = tile.T
            for quarter in range(4):
                target, c = 2 * h + quarter // 2, quarter % 2
                for piece in range(2):
                    at = g * 32 + piece * 16
                    first = quarter * 32 + piece * 16
                    half, at = at // HALF, at % HALF
                    p_t[c, half, place_of[half][target], at : at + 16, lanes] = turned[first : first + 16]
        return carry

    lax.fori_loop(0, TR, own_row, 0, unroll=4)

    for copy in early[2:]:
        copy.wait_recv()
    s_up = remote(s_send.at[1], s_halo.at[0], s_ssem.at[1], s_rsem.at[1], to_up)
    s_down = remote(s_send.at[0], s_halo.at[1], s_ssem.at[0], s_rsem.at[0], to_down)
    s_up.wait_recv()
    s_down.wait_recv()

    def halo_rows(j, carry):
        for region in range(2):
            tiles = [s0_halo[region, j]] + [s_halo[region, j, m] for m in range(K - 1)]
            lines = [pc_halo[region, m, pl.ds(j, 1), :] for m in range(K)]

            def factor(m, slot):
                ones = jnp.where(lines[m] == slot, 1.0, 0.0)
                block = jnp.broadcast_to(ones, (16, B)).astype(BF16)
                return jnp.concatenate([block] * (B // 16), axis=0)

            for slot in range(3 * NCG):
                g, h = slot // NCG, slot % NCG
                p_all[TR + region * GD + j, g + 2 * region, :, h * B : (h + 1) * B] = slot_tile(
                    tiles, factor, slot
                )
        return carry

    lax.fori_loop(0, GD, halo_rows, 0)

    def place_group(g):
        first = 0 if 1 <= g <= 3 else 1

        def place_row(row, carry):
            left = jnp.concatenate([a_v[row, k] for k in range(first, K)], axis=1)
            right = jnp.concatenate([p_all[cols_ref[k, row], g] for k in range(first, K)], axis=0)
            value = jnp.dot(left, right, preferred_element_type=F32)
            ap[g, pl.ds(pl.multiple_of(row * B, B), B), :] = value.astype(BF16)
            return carry

        lax.fori_loop(0, TR, place_row, 0, unroll=8)

    core_copies, x1_copies, x2_copies, y_copies = [], [], [], []

    def begin(copies, *args):
        copies.append(remote(*args))
        copies[-1].start()

    def product(n, c):
        left = p_t[c].reshape(8 * HALF, TR * B)
        value = jnp.dot(left, ap[n], preferred_element_type=F32)
        part[n, c] = value.reshape(2, 4, HALF, G)

    def core_stage(n):
        core_copies[n].wait_recv()
        q[n] = part[n, core] + core_in[n]
        for half, device in ((0, to_a), (1, to_b)):
            i = 2 * n + half
            begin(
                x1_copies, q.at[n, half, pl.ds(0, 2)], x1_in.at[n, half],
                x1_ssem.at[i], x1_rsem.at[i], device,
            )

    def x1_stage(n):
        for half, device in ((0, to_b), (1, to_a)):
            i = 2 * n + half
            x1_copies[i].wait_recv()
            x2_out[n, half] = q[n, half, 2] + x1_in[n, half, 0]
            begin(
                x2_copies, x2_out.at[n, half], x2_in.at[n, half],
                x2_ssem.at[i], x2_rsem.at[i], device,
            )

    def x2_stage(n):
        for half in range(2):
            x2_copies[2 * n + half].wait_recv()
            fin[n, half * HALF : (half + 1) * HALF] = q[n, half, 3] + x1_in[n, half, 1] + x2_in[n, half]
        for region, device in ((0, to_up), (1, to_down)):
            i = 2 * n + region
            begin(
                y_copies, fin.at[n, pl.ds(64 - 64 * region, 32)], y_in.at[n, region],
                y_ssem.at[i], y_rsem.at[i], device,
            )

    for n in range(5):
        place_group(n)
        if n >= 1:
            core_stage(n - 1)
        if n >= 2:
            x1_stage(n - 2)
        if n >= 3:
            x2_stage(n - 3)
        product(n, 1 - core)
        begin(core_copies, part.at[n, 1 - core], core_in.at[n], c_ssem.at[n], c_rsem.at[n], to_core)
        product(n, core)
    core_stage(4)
    x1_stage(3)
    x2_stage(2)
    x1_stage(4)
    x2_stage(3)
    x2_stage(4)
    for copy in y_copies:
        copy.wait_recv()
    for g in range(7):
        total = None
        for n, value in (
            (g - 1, lambda n: fin[n, 32:64]),
            (g, lambda n: jnp.where(dom > 0, y_in[n, 0], 0.0)),
            (g - 2, lambda n: jnp.where(dom < n_dom - 1, y_in[n, 1], 0.0)),
        ):
            if 0 <= n < 5:
                total = value(n) if total is None else total + value(n)
        out_ref[:, g * G : (g + 1) * G] = total

    for copy in early + [s_up, s_down] + core_copies + x1_copies + x2_copies + y_copies:
        copy.wait_send()


def on_device(a_vals, a_cols, send_rows, tentative, p_cols, ap_cols):
    hbm = pl.BlockSpec(memory_space=pl.ANY)
    smem = pl.BlockSpec(memory_space=pltpu.SMEM)
    dma = pltpu.SemaphoreType.DMA
    return pl.pallas_call(
        kernel,
        out_shape=jax.ShapeDtypeStruct((32, 7 * G), F32),
        in_specs=[hbm, smem, smem, hbm, smem],
        out_specs=pl.BlockSpec(memory_space=pltpu.VMEM),
        scratch_shapes=[
            pltpu.VMEM((TR, K, B, B), BF16),
            pltpu.VMEM((TR, B, B), BF16),
            pltpu.VMEM((TR + 2 * GD, B, B), BF16),
            pltpu.VMEM((2, GD, B, B), BF16),
            pltpu.VMEM((2, GD, B, B), BF16),
            pltpu.VMEM((2, GD, B, B), BF16),
            pltpu.VMEM((2, GD, K - 1, B, B), BF16),
            pltpu.VMEM((2, GD, K - 1, B, B), BF16),
            pltpu.VMEM((2, K, GD, B), jnp.int32),
            pltpu.VMEM((2, K, GD, B), jnp.int32),
            pltpu.VMEM((TR + 2 * GD, 5, B, G), BF16),
            pltpu.VMEM((2, 2, 4, HALF, TR * B), BF16),
            pltpu.VMEM((5, TR * B, G), BF16),
            pltpu.VMEM((5, 2, 2, 4, HALF, G), F32),
            pltpu.VMEM((5, 2, 4, HALF, G), F32),
            pltpu.VMEM((5, 2, 4, HALF, G), F32),
            pltpu.VMEM((5, 2, 2, HALF, G), F32),
            pltpu.VMEM((5, 2, HALF, G), F32),
            pltpu.VMEM((5, 2, HALF, G), F32),
            pltpu.VMEM((5, 2 * HALF, G), F32),
            pltpu.VMEM((5, 2, 32, G), F32),
            dma((3,)),
            dma((2,)), dma((2,)), dma((2,)), dma((2,)), dma((2,)), dma((2,)), dma((2,)), dma((2,)),
            dma((5,)), dma((5,)), dma((10,)), dma((10,)), dma((10,)), dma((10,)), dma((10,)), dma((10,)),
        ],
        compiler_params=pltpu.CompilerParams(
            collective_id=0, has_side_effects=True, vmem_limit_bytes=60 * 1024 * 1024
        ),
        cost_estimate=pl.CostEstimate(flops=16_000_000_000, bytes_accessed=8_000_000, transcendentals=0),
    )(a_vals, a_cols.T, send_rows.reshape(2, GD), tentative, p_cols.T)


def solution(mesh):
    placed = (
        P(("dom", "sub"), None, None, None),
        P(("dom", "sub"), None),
        P(("dom", "sub"), None, None),
        P(("dom", "sub"), None, None),
        P(("dom", "sub"), None),
        P(("dom", "sub"), None, None),
    )
    return jax.shard_map(
        on_device, mesh=mesh, in_specs=placed, out_specs=P(("dom", "sub"), None), check_vma=False
    )
```

time: 92.6 us -> 84.6 us (0.914)
  Pallas kernels: 88 us -> 82.8 us
  local copies, waits for them, and re-layouts: 4.37 us -> 1.64 us
    pallas_call x1, Pallas kernels: 88 us -> 82.8 us  [on_device(): pl.pallas_call(kernel, out_shape=jax.ShapeDtypeStruct((32, 7 * G), F32),...]
    unnamed x3 -> x1, local copies, waits for them, and re-layouts: 4.37 us -> 1.64 us
where the time goes in v2:
time: 84.6 us; the launch traced here: 84.5 us
  Pallas kernels  82.8 us (98%)
  local copies, waits for them, and re-layouts  1.64 us (2%)
    pallas_call x1, Pallas kernels, on_device(): pl.pallas_call(kernel, out_shape=jax.ShapeDtypeStruct((32, 7 * G), F32),...  82.8 us

profile of v2, /device:TPU:0, one launch (start us, length us, event | category | flops | bytes accessed | tf_op | source)
XLA Modules:
  0.0 84.5 jit_solution(11117075200609536521)
XLA Ops:
  0.0 82.8 %shard_map.55 = f32[32,1792]{1,0:T(8,128)} custom-call(bf16[32,4,128,128]{3,2,1,0:T(8,128)(2,1)} %a_hbm.1, s32[4,32]{1,0:T(4,128)} %bitcast.3, s32[2,8]{1,0:T(2,128)} %bitcast.5, bf16[32,128,128]{2,1,0:T(8,128)(2,1)} %t_hbm.1, s32[4,32]{1,0:T(4,128)} %bitcast.4), custom_call_target="tpu_custom_call" | custom-call | flops 16000000000 | bytes 8000000 | tf_op jit(solution)/shard_map/pallas_call | solution.py:299
  82.8 1.6 %copy.7 = f32[32,1792]{1,0:T(8,128)} copy(f32[32,1792]{1,0:T(8,128)} %shard_map.55) | data formatting | bytes 458752

commit v3 on v2

v3 whole, which is shorter than its diff:
```python
import jax
import jax.numpy as jnp
from jax import lax
from jax.experimental import pallas as pl
from jax.experimental.pallas import tpu as pltpu
from jax.sharding import PartitionSpec as P

B = 128
K = 4
TR = 32
NCG = 2
GD = 8
G = NCG * B
HB = B // 2
R3 = 96
OMEGA = 0.6
F32 = jnp.float32
BF16 = jnp.bfloat16
MESH = pl.DeviceIdType.MESH


def row_weight(a_v, row, eye):
    diagonal = jnp.sum(jnp.where(eye, a_v[row, 0].astype(F32), 0.0), axis=1, keepdims=True)
    return OMEGA * (1.0 / diagonal)


def smooth_tiles(a_v, t_ext, cols_ref, row, eye, first):
    weight = row_weight(a_v, row, eye)
    tiles = []
    for m in range(first, K):
        product = jnp.dot(a_v[row, m], t_ext[cols_ref[m, row]], preferred_element_type=F32)
        value = weight * product
        value = t_ext[row].astype(F32) - value if m == 0 else -value
        tiles.append(value.astype(BF16))
    return tiles


def doubled(tile, half):
    part = tile[:, half * HB : (half + 1) * HB]
    return jnp.concatenate([part, part], axis=1)


def paired(one, two, half):
    columns = slice(half * HB, (half + 1) * HB)
    return jnp.concatenate([one[:, columns], two[:, columns]], axis=1)


def group_tile(doubles, slots, group):
    wanted = NCG * group + (lax.broadcasted_iota(jnp.int32, (1, B), 1) >= HB).astype(jnp.int32)
    total = None
    for m in range(K):
        if m == 0 and group != 1:
            continue
        ones = jnp.where(slots[m] == wanted, 1.0, 0.0)
        block = jnp.broadcast_to(ones, (16, B)).astype(BF16)
        term = doubles[m] * jnp.concatenate([block] * (B // 16), axis=0)
        total = term if total is None else total + term
    return total


def chunk_of(half, group):
    return (4, half) if group == 4 else (2 * half + group // 2, group % 2)


def put(p_all, row, half, group, tile):
    chunk, at = chunk_of(half, group)
    p_all[row, chunk, :, at * B : (at + 1) * B] = tile


def clear_rows(p_all):
    empty = jnp.zeros((B, B), BF16)
    for first, count, groups in ((0, TR, (0, 4)), (TR, GD, (3, 4)), (TR + GD, GD, (0, 1))):

        def body(j, carry, first=first, groups=groups):
            for group in groups:
                for half in range(2):
                    put(p_all, first + j, half, group, empty)
            return carry

        lax.fori_loop(0, count, body, 0, unroll=2)


def identity_mask():
    return lax.broadcasted_iota(jnp.int32, (B, B), 0) == lax.broadcasted_iota(jnp.int32, (B, B), 1)


def first_tiles(a_v, t_own, lists_ref, s0_send):
    eye = identity_mask()

    def body(j, carry):
        for side in range(2):
            row = lists_ref[side, j]
            product = jnp.dot(a_v[row, 0], t_own[row], preferred_element_type=F32)
            value = t_own[row].astype(F32) - row_weight(a_v, row, eye) * product
            s0_send[side, j] = value.astype(BF16)
        return carry

    lax.fori_loop(0, GD, body, 0, unroll=4)


def send_rows(a_v, t_ext, cols_ref, lists_ref, s_send, start):
    eye = identity_mask()

    def body(pair, carry):
        for side in range(2):
            one, two = (
                smooth_tiles(a_v, t_ext, cols_ref, lists_ref[side, 2 * pair + e], eye, 1) for e in range(2)
            )
            for half in range(2):
                s_send[half, side, pair, 0] = paired(one[0], one[1], half)
                s_send[half, side, pair, 1] = paired(two[0], two[1], half)
                s_send[half, side, pair, 2] = paired(one[2], two[2], half)
            start(side, pair)
        return carry

    lax.fori_loop(0, GD // 2, body, 0, unroll=2)


def own_rows(a_v, t_ext, cols_ref, slots_ref, p_all, p_t, place_of):
    eye = identity_mask()

    def body(row, carry):
        tiles = smooth_tiles(a_v, t_ext, cols_ref, row, eye, 0)
        slots = [slots_ref[m, row] for m in range(K)]
        lanes = pl.ds(pl.multiple_of(row * B, B), B)
        for half in range(2):
            doubles = [doubled(tile, half) for tile in tiles]
            for group in range(3):
                tile = group_tile(doubles, slots, group)
                put(p_all, row, half, group + 1, tile)
                turned = tile.T
                for s in range(2):
                    for c in range(2):
                        first = s * HB + c * 32
                        p_t[c, place_of[2 * s + half], group * 32 : group * 32 + 32, lanes] = turned[
                            first : first + 32
                        ]
        return carry

    lax.fori_loop(0, TR, body, 0, unroll=4)


def halo_rows(half, s0_halo, s_halo, pc_halo, p_all):
    def body(pair, carry):
        for region in range(2):
            for e in range(2):
                j = 2 * pair + e
                both, third = s_halo[half, region, pair, e], s_halo[half, region, pair, 2]
                doubles = [
                    doubled(s0_halo[region, j], half), doubled(both, 0), doubled(both, 1), doubled(third, e),
                ]
                slots = [pc_halo[region, m, pl.ds(j, 1), :] for m in range(K)]
                for group in range(3):
                    put(
                        p_all, TR + region * GD + j, half, group + 2 * region,
                        group_tile(doubles, slots, group),
                    )
        return carry

    lax.fori_loop(0, GD // 2, body, 0)


def place_chunk(n, a_v, cols_ref, p_all, ap):
    first = 1 if n == 4 else 0

    def body(row, carry):
        left = jnp.concatenate([a_v[row, k] for k in range(first, K)], axis=1)
        right = jnp.concatenate([p_all[cols_ref[k, row], n] for k in range(first, K)], axis=0)
        value = jnp.dot(left, right, preferred_element_type=F32)
        ap[n, pl.ds(pl.multiple_of(row * B, B), B), :] = value.astype(BF16)
        return carry

    lax.fori_loop(0, TR, body, 0, unroll=16)


def product_chunk(n, c, p_t, ap, part):
    left = p_t[c].reshape(4 * R3, TR * B)
    value = jnp.dot(left, ap[n], preferred_element_type=F32)
    part[n, c] = value.reshape(4, R3, G)


def kernel(
    a_hbm, cols_ref, lists_ref, t_hbm, slots_ref, out_ref,
    a_v, t_own, t_ext, t_send, s0_send, s0_halo, s_send, s_halo, pc_send, pc_halo,
    p_all, p_t, ap, part, core_in, q, x_in, fin, y_in,
    load_sem, t_ssem, t_rsem, s0_ssem, s0_rsem, s_ssem, s_rsem, pc_ssem, pc_rsem,
    c_ssem, c_rsem, x_ssem, x_rsem, y_ssem, y_rsem,
):
    dom, sub = lax.axis_index("dom"), lax.axis_index("sub")
    n_dom = lax.axis_size("dom")
    up, down = lax.rem(dom + 1, n_dom), lax.rem(dom + n_dom - 1, n_dom)
    x, core = sub // 2, lax.rem(sub, 2)
    xa = x + 1 - 2 * lax.rem(x, 2)
    xb = 3 - x
    xo = lax.rem(x + 2, 4)
    to_up, to_down = (up, sub), (down, sub)
    to_core = (dom, 2 * x + 1 - core)
    to_ring = tuple((dom, 2 * chip + core) for chip in (xa, xb, xo))

    load_own = pltpu.make_async_copy(t_hbm, t_own, load_sem.at[0])
    load_ext = pltpu.make_async_copy(t_hbm, t_ext.at[pl.ds(0, TR)], load_sem.at[1])
    load_a = pltpu.make_async_copy(a_hbm, a_v, load_sem.at[2])
    load_own.start()
    load_a.start()
    load_ext.start()

    barrier = pltpu.get_barrier_semaphore()
    for device in (to_up, to_down, to_core) + to_ring:
        pl.semaphore_signal(barrier, inc=1, device_id=device, device_id_type=MESH)

    def remote(src, dst, ssem, rsem, device):
        return pltpu.make_async_remote_copy(
            src_ref=src, dst_ref=dst, send_sem=ssem, recv_sem=rsem,
            device_id=device, device_id_type=MESH,
        )

    load_own.wait()

    def gather_row(j, carry):
        for side in range(2):
            t_send[side, j] = t_own[lists_ref[side, j]]
        return carry

    lax.fori_loop(0, GD, gather_row, 0, unroll=4)

    for side in range(2):
        for j in range(GD):
            row = lists_ref[side, j]
            for m in range(K):
                pc_send[side, m, j : j + 1, :] = jnp.full((1, B), slots_ref[m, row], jnp.int32)

    load_a.wait()
    first_tiles(a_v, t_own, lists_ref, s0_send)
    pl.semaphore_wait(barrier, 6)

    early = []
    for send, halo, ssem, rsem in (
        (t_send, None, t_ssem, t_rsem), (pc_send, pc_halo, pc_ssem, pc_rsem), (s0_send, s0_halo, s0_ssem, s0_rsem),
    ):
        for region, device in ((0, to_up), (1, to_down)):
            target = t_ext.at[pl.ds(TR + GD * region, GD)] if halo is None else halo.at[region]
            early.append(remote(send.at[1 - region], target, ssem.at[region], rsem.at[region], device))
            early[-1].start()

    clear_rows(p_all)
    load_ext.wait()
    early[0].wait_recv()
    early[1].wait_recv()

    def start_pair(side, pair):
        remote(
            s_send.at[0, side, pair], s_halo.at[0, 1 - side, pair], s_ssem.at[0, side], s_rsem.at[0, side],
            to_up if side == 1 else to_down,
        ).start()

    send_rows(a_v, t_ext, cols_ref, lists_ref, s_send, start_pair)

    def side_copy(half, side):
        return remote(
            s_send.at[half, side], s_halo.at[half, 1 - side], s_ssem.at[half, side], s_rsem.at[half, side],
            to_up if side == 1 else to_down,
        )

    s_copies = [[side_copy(half, side) for side in range(2)] for half in range(2)]

    place_of = [
        jnp.where(t == xa, 0, jnp.where(t == xb, 1, jnp.where(t == xo, 2, 3))) for t in range(4)
    ]
    own_rows(a_v, t_ext, cols_ref, slots_ref, p_all, p_t, place_of)
    for copy in s_copies[1]:
        copy.start()

    core_copies, x_copies, y_copies = [], [], []

    def begin(copies, *args):
        copies.append(remote(*args))
        copies[-1].start()

    def core_stage(n):
        core_copies[n].wait_recv()
        q[n] = part[n, core] + core_in[n]
        for t in range(3):
            i = 3 * n + t
            begin(x_copies, q.at[n, t], x_in.at[n, t], x_ssem.at[i], x_rsem.at[i], to_ring[t])

    def x_stage(n):
        for t in range(3):
            x_copies[3 * n + t].wait_recv()
        fin[n] = (q[n, 3] + x_in[n, 0]) + (x_in[n, 1] + x_in[n, 2])
        for region, device in ((0, to_up), (1, to_down)):
            i = 2 * n + region
            begin(
                y_copies, fin.at[n, pl.ds(64 - 64 * region, 32)], y_in.at[n, region],
                y_ssem.at[i], y_rsem.at[i], device,
            )

    def place(n):
        place_chunk(n, a_v, cols_ref, p_all, ap)

    def product(n):
        product_chunk(n, 1 - core, p_t, ap, part)
        begin(core_copies, part.at[n, 1 - core], core_in.at[n], c_ssem.at[n], c_rsem.at[n], to_core)
        product_chunk(n, core, p_t, ap, part)

    for copy in early[2:] + s_copies[0]:
        copy.wait_recv()
    halo_rows(0, s0_halo, s_halo, pc_halo, p_all)
    place(0)
    product(0)
    place(1)
    core_stage(0)
    product(1)
    for copy in s_copies[1]:
        copy.wait_recv()
    halo_rows(1, s0_halo, s_halo, pc_halo, p_all)
    place(2)
    core_stage(1)
    product(2)
    place(3)
    core_stage(2)
    product(3)
    place(4)
    core_stage(3)
    x_stage(0)
    product(4)
    x_stage(1)
    core_stage(4)
    x_stage(2)
    x_stage(3)
    x_stage(4)
    for copy in y_copies:
        copy.wait_recv()

    def columns(array, half, group):
        chunk, at = chunk_of(half, group)
        return array(chunk)[:, at * B : (at + 1) * B]

    for g in range(7):
        halves = []
        for half in range(2):
            total = None
            for group, array in (
                (g - 1, lambda n: fin[n, 32:64]),
                (g, lambda n: jnp.where(dom > 0, y_in[n, 0], 0.0)),
                (g - 2, lambda n: jnp.where(dom < n_dom - 1, y_in[n, 1], 0.0)),
            ):
                if 0 <= group < 5:
                    value = columns(array, half, group)
                    total = value if total is None else total + value
            halves.append(total)
        for s in range(2):
            out_ref[:, g * G + s * B : g * G + (s + 1) * B] = paired(halves[0], halves[1], s)

    for copy in early + s_copies[0] + s_copies[1] + core_copies + x_copies + y_copies:
        copy.wait_send()


def on_device(a_vals, a_cols, send_rows, tentative, p_cols, ap_cols):
    hbm = pl.BlockSpec(memory_space=pl.ANY)
    smem = pl.BlockSpec(memory_space=pltpu.SMEM)
    dma = pltpu.SemaphoreType.DMA
    return pl.pallas_call(
        kernel,
        out_shape=jax.ShapeDtypeStruct((32, 7 * G), F32),
        in_specs=[hbm, smem, smem, hbm, smem],
        out_specs=pl.BlockSpec(memory_space=pltpu.VMEM),
        scratch_shapes=[
            pltpu.VMEM((TR, K, B, B), BF16),
            pltpu.VMEM((TR, B, B), BF16),
            pltpu.VMEM((TR + 2 * GD, B, B), BF16),
            pltpu.VMEM((2, GD, B, B), BF16),
            pltpu.VMEM((2, GD, B, B), BF16),
            pltpu.VMEM((2, GD, B, B), BF16),
            pltpu.VMEM((2, 2, GD // 2, K - 1, B, B), BF16),
            pltpu.VMEM((2, 2, GD // 2, K - 1, B, B), BF16),
            pltpu.VMEM((2, K, GD, B), jnp.int32),
            pltpu.VMEM((2, K, GD, B), jnp.int32),
            pltpu.VMEM((TR + 2 * GD, 5, B, G), BF16),
            pltpu.VMEM((2, 4, R3, TR * B), BF16),
            pltpu.VMEM((5, TR * B, G), BF16),
            pltpu.VMEM((5, 2, 4, R3, G), F32),
            pltpu.VMEM((5, 4, R3, G), F32),
            pltpu.VMEM((5, 4, R3, G), F32),
            pltpu.VMEM((5, 3, R3, G), F32),
            pltpu.VMEM((5, R3, G), F32),
            pltpu.VMEM((5, 2, 32, G), F32),
            dma((3,)),
            dma((2,)), dma((2,)), dma((2,)), dma((2,)), dma((2, 2)), dma((2, 2)), dma((2,)), dma((2,)),
            dma((5,)), dma((5,)), dma((15,)), dma((15,)), dma((10,)), dma((10,)),
        ],
        compiler_params=pltpu.CompilerParams(
            collective_id=0, has_side_effects=True, vmem_limit_bytes=60 * 1024 * 1024
        ),
        cost_estimate=pl.CostEstimate(flops=16_000_000_000, bytes_accessed=8_000_000, transcendentals=0),
    )(a_vals, a_cols.T, send_rows.reshape(2, GD), tentative, p_cols.T)


def solution(mesh):
    placed = (
        P(("dom", "sub"), None, None, None),
        P(("dom", "sub"), None),
        P(("dom", "sub"), None, None),
        P(("dom", "sub"), None, None),
        P(("dom", "sub"), None),
        P(("dom", "sub"), None, None),
    )
    return jax.shard_map(
        on_device, mesh=mesh, in_specs=placed, out_specs=P(("dom", "sub"), None), check_vma=False
    )
```

time: 84.6 us -> 74.1 us (0.88)
  Pallas kernels: 82.8 us -> 72.3 us
    pallas_call x1, Pallas kernels: 82.8 us -> 72.3 us  [on_device(): pl.pallas_call(kernel, out_shape=jax.ShapeDtypeStruct((32, 7 * G), F32),...]
where the time goes in v3:
time: 74.1 us; the launch traced here: 74 us
  Pallas kernels  72.3 us (98%)
  local copies, waits for them, and re-layouts  1.64 us (2%)
    pallas_call x1, Pallas kernels, on_device(): pl.pallas_call(kernel, out_shape=jax.ShapeDtypeStruct((32, 7 * G), F32),...  72.3 us
    unnamed x1, local copies, waits for them, and re-layouts  1.64 us

profile of v3, /device:TPU:0, one launch (start us, length us, event | category | flops | bytes accessed | tf_op | source)
XLA Modules:
  0.0 74.0 jit_solution(11756612564382777098)
XLA Ops:
  0.0 72.3 %shard_map.55 = f32[32,1792]{1,0:T(8,128)} custom-call(bf16[32,4,128,128]{3,2,1,0:T(8,128)(2,1)} %a_hbm.1, s32[4,32]{1,0:T(4,128)} %bitcast.3, s32[2,8]{1,0:T(2,128)} %bitcast.5, bf16[32,128,128]{2,1,0:T(8,128)(2,1)} %t_hbm.1, s32[4,32]{1,0:T(4,128)} %bitcast.4), custom_call_target="tpu_custom_call" | custom-call | flops 16000000000 | bytes 8000000 | tf_op jit(solution)/shard_map/pallas_call | solution.py:362
  72.3 1.6 %copy.7 = f32[32,1792]{1,0:T(8,128)} copy(f32[32,1792]{1,0:T(8,128)} %shard_map.55) | data formatting | bytes 458752

commit v4 on v3

--- a/solution.py
+++ b/solution.py
@@ -179,10 +179,28 @@
     part[n, c] = value.reshape(4, R3, G)
 
 
+STEPS = 32000.0
+LIFT = 10
+
+
+def encode(block, coded):
+    top = jnp.max(jnp.abs(block), axis=0, keepdims=True)
+    exponent = jnp.clip(jnp.ceil(jnp.log2(jnp.maximum(top, 1e-37))), -116.0, 128.0)
+    scaled = (block * jnp.exp2(LIFT - exponent)) * (STEPS / 2**LIFT)
+    coded[:R3] = jnp.round(scaled).astype(jnp.int32).astype(jnp.int16)
+    coded[R3:] = jnp.broadcast_to(exponent, (16, G)).astype(jnp.int32).astype(jnp.int16)
+
+
+def decode(coded):
+    exponent = coded[R3:].astype(jnp.int32).astype(F32)[:1]
+    values = coded[:R3].astype(jnp.int32).astype(F32)
+    return (values * (2**LIFT / STEPS)) * jnp.exp2(exponent - LIFT)
+
+
 def kernel(
     a_hbm, cols_ref, lists_ref, t_hbm, slots_ref, out_ref,
     a_v, t_own, t_ext, t_send, s0_send, s0_halo, s_send, s_halo, pc_send, pc_halo,
-    p_all, p_t, ap, part, core_in, q, x_in, fin, y_in,
+    p_all, p_t, ap, part, core_in, q, x_out, x_in, fin, y_in,
     load_sem, t_ssem, t_rsem, s0_ssem, s0_rsem, s_ssem, s_rsem, pc_ssem, pc_rsem,
     c_ssem, c_rsem, x_ssem, x_rsem, y_ssem, y_rsem,
 ):
@@ -270,7 +288,7 @@
     for copy in s_copies[1]:
         copy.start()
 
-    core_copies, x_copies, y_copies = [], [], []
+    core_copies, x_copies, y_copies = [], [None] * 15, []
 
     def begin(copies, *args):
         copies.append(remote(*args))
@@ -278,15 +296,17 @@
 
     def core_stage(n):
         core_copies[n].wait_recv()
-        q[n] = part[n, core] + core_in[n]
-        for t in range(3):
+        for t in (2, 0, 1):
             i = 3 * n + t
-            begin(x_copies, q.at[n, t], x_in.at[n, t], x_ssem.at[i], x_rsem.at[i], to_ring[t])
+            encode(part[n, core, t] + core_in[n, t], x_out.at[n, t])
+            x_copies[i] = remote(x_out.at[n, t], x_in.at[n, t], x_ssem.at[i], x_rsem.at[i], to_ring[t])
+            x_copies[i].start()
+        q[n] = part[n, core, 3] + core_in[n, 3]
 
     def x_stage(n):
         for t in range(3):
             x_copies[3 * n + t].wait_recv()
-        fin[n] = (q[n, 3] + x_in[n, 0]) + (x_in[n, 1] + x_in[n, 2])
+        fin[n] = (q[n] + decode(x_in.at[n, 0])) + (decode(x_in.at[n, 1]) + decode(x_in.at[n, 2]))
         for region, device in ((0, to_up), (1, to_down)):
             i = 2 * n + region
             begin(
@@ -298,9 +318,9 @@
         place_chunk(n, a_v, cols_ref, p_all, ap)
 
     def product(n):
-        product_chunk(n, 1 - core, p_t, ap, part)
+        for c in range(2):
+            product_chunk(n, c, p_t, ap, part)
         begin(core_copies, part.at[n, 1 - core], core_in.at[n], c_ssem.at[n], c_rsem.at[n], to_core)
-        product_chunk(n, core, p_t, ap, part)
 
     for copy in early[2:] + s_copies[0]:
         copy.wait_recv()
@@ -380,8 +400,9 @@
             pltpu.VMEM((5, TR * B, G), BF16),
             pltpu.VMEM((5, 2, 4, R3, G), F32),
             pltpu.VMEM((5, 4, R3, G), F32),
-            pltpu.VMEM((5, 4, R3, G), F32),
-            pltpu.VMEM((5, 3, R3, G), F32),
+            pltpu.VMEM((5, R3, G), F32),
+            pltpu.VMEM((5, 3, R3 + 16, G), jnp.int16),
+            pltpu.VMEM((5, 3, R3 + 16, G), jnp.int16),
             pltpu.VMEM((5, R3, G), F32),
             pltpu.VMEM((5, 2, 32, G), F32),
             dma((3,)),

time: 74.1 us -> 66.1 us (0.89)
  Pallas kernels: 72.3 us -> 64.3 us
    pallas_call x1, Pallas kernels: 72.3 us -> 64.3 us  [on_device(): pl.pallas_call(kernel, out_shape=jax.ShapeDtypeStruct((32, 7 * G), F32),...]
where the time goes in v4:
time: 66.1 us; the launch traced here: 65.9 us
  Pallas kernels  64.3 us (97%)
  local copies, waits for them, and re-layouts  1.64 us (2%)
    pallas_call x1, Pallas kernels, on_device(): pl.pallas_call(kernel, out_shape=jax.ShapeDtypeStruct((32, 7 * G), F32),...  64.3 us
    unnamed x1, local copies, waits for them, and re-layouts  1.64 us

profile of v4, /device:TPU:0, one launch (start us, length us, event | category | flops | bytes accessed | tf_op | source)
XLA Modules:
  0.0 65.9 jit_solution(8302158683579042693)
XLA Ops:
  0.0 64.3 %shard_map.55 = f32[32,1792]{1,0:T(8,128)} custom-call(bf16[32,4,128,128]{3,2,1,0:T(8,128)(2,1)} %a_hbm.1, s32[4,32]{1,0:T(4,128)} %bitcast.3, s32[2,8]{1,0:T(2,128)} %bitcast.5, bf16[32,128,128]{2,1,0:T(8,128)(2,1)} %t_hbm.1, s32[4,32]{1,0:T(4,128)} %bitcast.4), custom_call_target="tpu_custom_call" | custom-call | flops 16000000000 | bytes 8000000 | tf_op jit(solution)/shard_map/pallas_call | solution.py:382
  64.3 1.6 %copy.7 = f32[32,1792]{1,0:T(8,128)} copy(f32[32,1792]{1,0:T(8,128)} %shard_map.55) | data formatting | bytes 458752

commit v5 on v4

--- a/solution.py
+++ b/solution.py
@@ -113,7 +113,7 @@
             start(side, pair)
         return carry
 
-    lax.fori_loop(0, GD // 2, body, 0, unroll=2)
+    lax.fori_loop(0, GD // 2, body, 0, unroll=4)
 
 
 def own_rows(a_v, t_ext, cols_ref, slots_ref, p_all, p_t, place_of):
@@ -149,7 +149,8 @@
                 doubles = [
                     doubled(s0_halo[region, j], half), doubled(both, 0), doubled(both, 1), doubled(third, e),
                 ]
-                slots = [pc_halo[region, m, pl.ds(j, 1), :] for m in range(K)]
+                line = pc_halo[region, pl.ds(j, 1), :]
+                slots = [jnp.broadcast_to(line[:, m : m + 1], (1, B)) for m in range(K)]
                 for group in range(3):
                     put(
                         p_all, TR + region * GD + j, half, group + 2 * region,
@@ -157,7 +158,7 @@
                     )
         return carry
 
-    lax.fori_loop(0, GD // 2, body, 0)
+    lax.fori_loop(0, GD // 2, body, 0, unroll=4)
 
 
 def place_chunk(n, a_v, cols_ref, p_all, ap):
@@ -170,7 +171,7 @@
         ap[n, pl.ds(pl.multiple_of(row * B, B), B), :] = value.astype(BF16)
         return carry
 
-    lax.fori_loop(0, TR, body, 0, unroll=16)
+    lax.fori_loop(0, TR, body, 0, unroll=32)
 
 
 def product_chunk(n, c, p_t, ap, part):
@@ -215,6 +216,10 @@
     to_core = (dom, 2 * x + 1 - core)
     to_ring = tuple((dom, 2 * chip + core) for chip in (xa, xb, xo))
 
+    barrier = pltpu.get_barrier_semaphore()
+    for device in (to_up, to_down, to_core) + to_ring:
+        pl.semaphore_signal(barrier, inc=1, device_id=device, device_id_type=MESH)
+
     load_own = pltpu.make_async_copy(t_hbm, t_own, load_sem.at[0])
     load_ext = pltpu.make_async_copy(t_hbm, t_ext.at[pl.ds(0, TR)], load_sem.at[1])
     load_a = pltpu.make_async_copy(a_hbm, a_v, load_sem.at[2])
@@ -222,10 +227,6 @@
     load_a.start()
     load_ext.start()
 
-    barrier = pltpu.get_barrier_semaphore()
-    for device in (to_up, to_down, to_core) + to_ring:
-        pl.semaphore_signal(barrier, inc=1, device_id=device, device_id_type=MESH)
-
     def remote(src, dst, ssem, rsem, device):
         return pltpu.make_async_remote_copy(
             src_ref=src, dst_ref=dst, send_sem=ssem, recv_sem=rsem,
@@ -241,11 +242,14 @@
 
     lax.fori_loop(0, GD, gather_row, 0, unroll=4)
 
+    lane = lax.broadcasted_iota(jnp.int32, (1, B), 1)
     for side in range(2):
         for j in range(GD):
             row = lists_ref[side, j]
-            for m in range(K):
-                pc_send[side, m, j : j + 1, :] = jnp.full((1, B), slots_ref[m, row], jnp.int32)
+            line = jnp.full((1, B), slots_ref[0, row], jnp.int32)
+            for m in range(1, K):
+                line = jnp.where(lane == m, slots_ref[m, row], line)
+            pc_send[side, j : j + 1, :] = line
 
     load_a.wait()
     first_tiles(a_v, t_own, lists_ref, s0_send)
@@ -297,8 +301,9 @@
     def core_stage(n):
         core_copies[n].wait_recv()
         for t in (2, 0, 1):
+            encode(part[n, core, t] + core_in[n, t], x_out.at[n, t])
+        for t in (2, 0, 1):
             i = 3 * n + t
-            encode(part[n, core, t] + core_in[n, t], x_out.at[n, t])
             x_copies[i] = remote(x_out.at[n, t], x_in.at[n, t], x_ssem.at[i], x_rsem.at[i], to_ring[t])
             x_copies[i].start()
         q[n] = part[n, core, 3] + core_in[n, 3]
@@ -306,12 +311,15 @@
     def x_stage(n):
         for t in range(3):
             x_copies[3 * n + t].wait_recv()
-        fin[n] = (q[n] + decode(x_in.at[n, 0])) + (decode(x_in.at[n, 1]) + decode(x_in.at[n, 2]))
+        total = (q[n] + decode(x_in.at[n, 0])) + (decode(x_in.at[n, 1]) + decode(x_in.at[n, 2]))
+        fin[1, n], fin[2, n], fin[0, n] = total[:32], total[32:64], total[64:]
+
+    def y_stage(first, count):
+        chunks = pl.ds(first, count)
         for region, device in ((0, to_up), (1, to_down)):
-            i = 2 * n + region
+            i = 2 * first + region
             begin(
-                y_copies, fin.at[n, pl.ds(64 - 64 * region, 32)], y_in.at[n, region],
-                y_ssem.at[i], y_rsem.at[i], device,
+                y_copies, fin.at[region, chunks], y_in.at[region, chunks], y_ssem.at[i], y_rsem.at[i], device
             )
 
     def place(n):
@@ -341,13 +349,17 @@
     product(3)
     place(4)
     core_stage(3)
+    product(4)
     x_stage(0)
-    product(4)
+    core_stage(4)
     x_stage(1)
-    core_stage(4)
     x_stage(2)
     x_stage(3)
+    y_stage(0, 4)
     x_stage(4)
+    y_stage(4, 1)
+    for copy in early + s_copies[0] + s_copies[1] + core_copies + x_copies + y_copies:
+        copy.wait_send()
     for copy in y_copies:
         copy.wait_recv()
 
@@ -360,9 +372,9 @@
         for half in range(2):
             total = None
             for group, array in (
-                (g - 1, lambda n: fin[n, 32:64]),
-                (g, lambda n: jnp.where(dom > 0, y_in[n, 0], 0.0)),
-                (g - 2, lambda n: jnp.where(dom < n_dom - 1, y_in[n, 1], 0.0)),
+                (g - 1, lambda n: fin[2, n]),
+                (g, lambda n: jnp.where(dom > 0, y_in[0, n], 0.0)),
+                (g - 2, lambda n: jnp.where(dom < n_dom - 1, y_in[1, n], 0.0)),
             ):
                 if 0 <= group < 5:
                     value = columns(array, half, group)
@@ -370,9 +382,6 @@
             halves.append(total)
         for s in range(2):
             out_ref[:, g * G + s * B : g * G + (s + 1) * B] = paired(halves[0], halves[1], s)
-
-    for copy in early + s_copies[0] + s_copies[1] + core_copies + x_copies + y_copies:
-        copy.wait_send()
 
 
 def on_device(a_vals, a_cols, send_rows, tentative, p_cols, ap_cols):
@@ -393,8 +402,8 @@
             pltpu.VMEM((2, GD, B, B), BF16),
             pltpu.VMEM((2, 2, GD // 2, K - 1, B, B), BF16),
             pltpu.VMEM((2, 2, GD // 2, K - 1, B, B), BF16),
-            pltpu.VMEM((2, K, GD, B), jnp.int32),
-            pltpu.VMEM((2, K, GD, B), jnp.int32),
+            pltpu.VMEM((2, GD, B), jnp.int32),
+            pltpu.VMEM((2, GD, B), jnp.int32),
             pltpu.VMEM((TR + 2 * GD, 5, B, G), BF16),
             pltpu.VMEM((2, 4, R3, TR * B), BF16),
             pltpu.VMEM((5, TR * B, G), BF16),
@@ -403,8 +412,8 @@
             pltpu.VMEM((5, R3, G), F32),
             pltpu.VMEM((5, 3, R3 + 16, G), jnp.int16),
             pltpu.VMEM((5, 3, R3 + 16, G), jnp.int16),
-            pltpu.VMEM((5, R3, G), F32),
-            pltpu.VMEM((5, 2, 32, G), F32),
+            pltpu.VMEM((3, 5, 32, G), F32),
+            pltpu.VMEM((2, 5, 32, G), F32),
             dma((3,)),
             dma((2,)), dma((2,)), dma((2,)), dma((2,)), dma((2, 2)), dma((2, 2)), dma((2,)), dma((2,)),
             dma((5,)), dma((5,)), dma((15,)), dma((15,)), dma((10,)), dma((10,)),

time: 66.1 us -> 65.1 us (0.985)
  Pallas kernels: 64.3 us -> 63.3 us
    pallas_call x1, Pallas kernels: 64.3 us -> 63.3 us  [on_device(): pl.pallas_call(kernel, out_shape=jax.ShapeDtypeStruct((32, 7 * G), F32),...]
where the time goes in v5:
time: 65.1 us; the launch traced here: 65 us
  Pallas kernels  63.3 us (97%)
  local copies, waits for them, and re-layouts  1.64 us (3%)
    pallas_call x1, Pallas kernels, on_device(): pl.pallas_call(kernel, out_shape=jax.ShapeDtypeStruct((32, 7 * G), F32),...  63.3 us
    unnamed x1, local copies, waits for them, and re-layouts  1.64 us

profile of v5, /device:TPU:0, one launch (start us, length us, event | category | flops | bytes accessed | tf_op | source)
XLA Modules:
  0.0 65.0 jit_solution(10168011265932892017)
XLA Ops:
  0.0 63.3 %shard_map.55 = f32[32,1792]{1,0:T(8,128)} custom-call(bf16[32,4,128,128]{3,2,1,0:T(8,128)(2,1)} %a_hbm.1, s32[4,32]{1,0:T(4,128)} %bitcast.3, s32[2,8]{1,0:T(2,128)} %bitcast.5, bf16[32,128,128]{2,1,0:T(8,128)(2,1)} %t_hbm.1, s32[4,32]{1,0:T(4,128)} %bitcast.4), custom_call_target="tpu_custom_call" | custom-call | flops 16000000000 | bytes 8000000 | tf_op jit(solution)/shard_map/pallas_call | solution.py:391
  63.3 1.6 %copy.7 = f32[32,1792]{1,0:T(8,128)} copy(f32[32,1792]{1,0:T(8,128)} %shard_map.55) | data formatting | bytes 458752

commit v6 on v5

--- a/solution.py
+++ b/solution.py
@@ -199,8 +199,8 @@
 
 
 def kernel(
-    a_hbm, cols_ref, lists_ref, t_hbm, slots_ref, out_ref,
-    a_v, t_own, t_ext, t_send, s0_send, s0_halo, s_send, s_halo, pc_send, pc_halo,
+    a_hbm, cols_hbm, lists_hbm, t_hbm, slots_hbm, out_ref,
+    cols_ref, lists_ref, slots_ref, a_v, t_own, t_ext, t_send, s0_send, s0_halo, s_send, s_halo, pc_send, pc_halo,
     p_all, p_t, ap, part, core_in, q, x_out, x_in, fin, y_in,
     load_sem, t_ssem, t_rsem, s0_ssem, s0_rsem, s_ssem, s_rsem, pc_ssem, pc_rsem,
     c_ssem, c_rsem, x_ssem, x_rsem, y_ssem, y_rsem,
@@ -223,7 +223,13 @@
     load_own = pltpu.make_async_copy(t_hbm, t_own, load_sem.at[0])
     load_ext = pltpu.make_async_copy(t_hbm, t_ext.at[pl.ds(0, TR)], load_sem.at[1])
     load_a = pltpu.make_async_copy(a_hbm, a_v, load_sem.at[2])
+    load_lists = pltpu.make_async_copy(lists_hbm, lists_ref, load_sem.at[3])
+    load_cols = pltpu.make_async_copy(cols_hbm, cols_ref, load_sem.at[4])
+    load_slots = pltpu.make_async_copy(slots_hbm, slots_ref, load_sem.at[5])
+    load_lists.start()
     load_own.start()
+    load_cols.start()
+    load_slots.start()
     load_a.start()
     load_ext.start()
 
@@ -233,6 +239,9 @@
             device_id=device, device_id_type=MESH,
         )
 
+    load_lists.wait()
+    load_cols.wait()
+    load_slots.wait()
     load_own.wait()
 
     def gather_row(j, carry):
@@ -386,14 +395,14 @@
 
 def on_device(a_vals, a_cols, send_rows, tentative, p_cols, ap_cols):
     hbm = pl.BlockSpec(memory_space=pl.ANY)
-    smem = pl.BlockSpec(memory_space=pltpu.SMEM)
     dma = pltpu.SemaphoreType.DMA
     return pl.pallas_call(
         kernel,
         out_shape=jax.ShapeDtypeStruct((32, 7 * G), F32),
-        in_specs=[hbm, smem, smem, hbm, smem],
+        in_specs=[hbm] * 5,
         out_specs=pl.BlockSpec(memory_space=pltpu.VMEM),
         scratch_shapes=[
+            pltpu.SMEM((K, TR), jnp.int32), pltpu.SMEM((2, GD), jnp.int32), pltpu.SMEM((K, TR), jnp.int32),
             pltpu.VMEM((TR, K, B, B), BF16),
             pltpu.VMEM((TR, B, B), BF16),
             pltpu.VMEM((TR + 2 * GD, B, B), BF16),
@@ -414,7 +423,7 @@
             pltpu.VMEM((5, 3, R3 + 16, G), jnp.int16),
             pltpu.VMEM((3, 5, 32, G), F32),
             pltpu.VMEM((2, 5, 32, G), F32),
-            dma((3,)),
+            dma((6,)),
             dma((2,)), dma((2,)), dma((2,)), dma((2,)), dma((2, 2)), dma((2, 2)), dma((2,)), dma((2,)),
             dma((5,)), dma((5,)), dma((15,)), dma((15,)), dma((10,)), dma((10,)),
         ],

time: 65.1 us -> 64.3 us (0.988)
  Pallas kernels: 63.3 us -> 62.6 us
    pallas_call x1, Pallas kernels: 63.3 us -> 62.6 us  [on_device(): pl.pallas_call(kernel, out_shape=jax.ShapeDtypeStruct((32, 7 * G), F32),...]
where the time goes in v6:
time: 64.3 us; the launch traced here: 64.2 us
  Pallas kernels  62.6 us (97%)
  local copies, waits for them, and re-layouts  1.64 us (3%)
    pallas_call x1, Pallas kernels, on_device(): pl.pallas_call(kernel, out_shape=jax.ShapeDtypeStruct((32, 7 * G), F32),...  62.6 us
    unnamed x1, local copies, waits for them, and re-layouts  1.64 us

profile of v6, /device:TPU:0, one launch (start us, length us, event | category | flops | bytes accessed | tf_op | source)
XLA Modules:
  0.0 64.2 jit_solution(16505179895161208418)
XLA Ops:
  0.0 62.6 %shard_map.55 = f32[32,1792]{1,0:T(8,128)} custom-call(bf16[32,4,128,128]{3,2,1,0:T(8,128)(2,1)} %a_hbm.1, s32[4,32]{1,0:T(4,128)} %bitcast.3, s32[2,8]{1,0:T(2,128)} %bitcast.5, bf16[32,128,128]{2,1,0:T(8,128)(2,1)} %t_hbm.1, s32[4,32]{1,0:T(4,128)} %bitcast.4), custom_call_target="tpu_custom_call" | custom-call | flops 16000000000 | bytes 8000000 | tf_op jit(solution)/shard_map/pallas_call | solution.py:399
  62.6 1.6 %copy.7 = f32[32,1792]{1,0:T(8,128)} copy(f32[32,1792]{1,0:T(8,128)} %shard_map.55) | data formatting | bytes 458752

commit v7 on v6

--- a/solution.py
+++ b/solution.py
@@ -240,8 +240,6 @@
         )
 
     load_lists.wait()
-    load_cols.wait()
-    load_slots.wait()
     load_own.wait()
 
     def gather_row(j, carry):
@@ -252,6 +250,7 @@
     lax.fori_loop(0, GD, gather_row, 0, unroll=4)
 
     lane = lax.broadcasted_iota(jnp.int32, (1, B), 1)
+    load_slots.wait()
     for side in range(2):
         for j in range(GD):
             row = lists_ref[side, j]
@@ -275,6 +274,7 @@
 
     clear_rows(p_all)
     load_ext.wait()
+    load_cols.wait()
     early[0].wait_recv()
     early[1].wait_recv()
 

time: 64.3 us -> 64.3 us (level)
  no operation moved by 1% of the time
where the time goes in v7:
time: 64.3 us; the launch traced here: 64.2 us
  Pallas kernels  62.6 us (97%)
  local copies, waits for them, and re-layouts  1.64 us (3%)
    pallas_call x1, Pallas kernels, on_device(): pl.pallas_call(kernel, out_shape=jax.ShapeDtypeStruct((32, 7 * G), F32),...  62.6 us
    unnamed x1, local copies, waits for them, and re-layouts  1.64 us

profile of v7, /device:TPU:0, one launch (start us, length us, event | category | flops | bytes accessed | tf_op | source)
XLA Modules:
  0.0 64.2 jit_solution(10677107627759973451)
XLA Ops:
  0.0 62.6 %shard_map.55 = f32[32,1792]{1,0:T(8,128)} custom-call(bf16[32,4,128,128]{3,2,1,0:T(8,128)(2,1)} %a_hbm.1, s32[4,32]{1,0:T(4,128)} %bitcast.3, s32[2,8]{1,0:T(2,128)} %bitcast.5, bf16[32,128,128]{2,1,0:T(8,128)(2,1)} %t_hbm.1, s32[4,32]{1,0:T(4,128)} %bitcast.4), custom_call_target="tpu_custom_call" | custom-call | flops 16000000000 | bytes 8000000 | tf_op jit(solution)/shard_map/pallas_call | solution.py:399
  62.6 1.6 %copy.7 = f32[32,1792]{1,0:T(8,128)} copy(f32[32,1792]{1,0:T(8,128)} %shard_map.55) | data formatting | bytes 458752
